TPU v7x, 512 devices: a whole 4x8x8 slice. The times are simulated.
512 devices in a mesh: grow: 64 (over x, z_lo, y), lat: 8 (over z_hi, core).
Axes of the slice: x: 4, y: 8, z: 8 (z_hi: 4, z_lo: 2; z = z_hi * 2 + z_lo), core: 2. Of those that a mesh axis runs over, the one named last changes fastest.
Arguments:
- labels: int32 [512, 256, 256], P('grow', 'lat'), may hold values from 0 to 3
- seed_blend: float32 [4, 512, 256, 256], P(None, 'grow', 'lat'), may hold values from 0.02 to 0.6
- potential: float32 [2, 512, 256, 256], P(None, 'grow', 'lat'), may hold values from -3 to 3
- inflow_index: int32 [8, 256, 256], P(None, 'lat'), may hold values from 0 to 15
- liquid_table: float32 [16, 2], replicated, may hold values from -1 to 1
Outputs:
- phase_field: float32 [4, 512, 256, 256], P(None, 'grow', 'lat')
- chem_field: float32 [2, 512, 256, 256], P(None, 'grow', 'lat')
All inputs are finite; a program needn't handle non-finite values.
Results may differ from a plain program's by a relative error of at most 0.0001.
Values sent between devices are 32-bit elements; how exact they have to be, the bound alone decides.
No kernel may reach another device: no remote copies, remote signals or barrier semaphores. Data moves between devices by JAX's collectives and lax.ppermute only.
A program may use at most 64 MiB of HBM per device.

v0:
```python
import jax
import jax.numpy as jnp
from jax import lax
from jax.sharding import PartitionSpec as P

offset_table = ((0.0, 0.0), (0.6, -0.3), (-0.4, 0.5), (-0.2, -0.6))
latent_heat = (0.0, 0.8, 0.8, 0.8)
relax_rate = 0.1
diffusion = 0.05


def passed_along(block, axis, distance):
    devices = range(lax.axis_size(axis))
    route = [(i - distance, i) for i in devices if i - distance in devices]
    return lax.ppermute(block, axis, route)


def with_halo(array, sides, width):
    for axis, dim in sides:
        count, length = (lax.axis_size(axis), array.shape[dim])
        up = [(i, (i + 1) % count) for i in range(count)]
        down = [(j, i) for i, j in up]
        last = lax.slice_in_dim(array, length - width, length, axis=dim)
        first = lax.slice_in_dim(array, 0, width, axis=dim)
        before = lax.ppermute(last, axis, up)
        after = lax.ppermute(first, axis, down)
        array = jnp.concatenate([before, array, after], axis=dim)
    return array


def evolve_fields(padded_fields, thermal_profile):
    centre = padded_fields[:, 1:-1, 1:-1]
    laplace = (
        padded_fields[:, 2:, 1:-1]
        + padded_fields[:, :-2, 1:-1]
        + (padded_fields[:, 1:-1, 2:] + padded_fields[:, 1:-1, :-2])
    )
    laplace = laplace + (jnp.roll(centre, -1, axis=3) + jnp.roll(centre, 1, axis=3)) - 6.0 * centre
    phases = centre[:4]
    chemical = centre[4:]
    offsets = jnp.array(offset_table, jnp.float32)
    latent_release = jnp.array(latent_heat, jnp.float32)[:, None, None, None]
    free_energy_density = jnp.zeros_like(phases)
    for solute in range(2):
        shifted = chemical[solute][None] + offsets[:, solute][:, None, None, None]
        free_energy_density = free_energy_density + shifted * shifted
    free_energy_density = -0.5 * free_energy_density + latent_release * thermal_profile
    driving = (
        laplace[:4]
        - phases * (1.0 - phases) * (1.0 - 2.0 * phases)
        - 2.0 * phases * free_energy_density
    )
    driving = driving - jnp.mean(driving, axis=0, keepdims=True)
    new_phases = phases + relax_rate * driving
    growth = new_phases * new_phases - phases * phases
    susceptible = jnp.sum(new_phases * new_phases, axis=0)
    mobile = diffusion * (0.1 + new_phases[0] * new_phases[0])
    new_chemical = []
    for solute in range(2):
        shifted = chemical[solute][None] + offsets[:, solute][:, None, None, None]
        source = jnp.sum(shifted * growth, axis=0)
        new_chemical.append(
            chemical[solute] + (mobile * laplace[4 + solute] - source) / susceptible
        )
    return jnp.concatenate([new_phases, jnp.stack(new_chemical)], axis=0)


def initial(labels, seed_blend, potential):
    kinds = jnp.arange(4, dtype=jnp.int32)[:, None, None, None]
    onehot = (labels[None] == kinds).astype(jnp.float32)
    phases = (onehot + seed_blend) / (1.0 + jnp.sum(seed_blend, axis=0))
    return jnp.concatenate([phases, potential], axis=0)


def inflow_fields(inflow_index, liquid_table):
    kinds = jnp.arange(liquid_table.shape[0], dtype=jnp.int32)[:, None, None, None]
    selected = (inflow_index[None] == kinds).astype(jnp.float32)
    chemical = []
    for solute in range(2):
        chemical.append(jnp.sum(selected * liquid_table[:, solute][:, None, None, None], axis=0))
    liquid = jnp.ones_like(chemical[0])
    solid = jnp.zeros_like(chemical[0])
    return jnp.stack([liquid, solid, solid, solid, chemical[0], chemical[1]])


def fix_ends(padded_fields, border_margin, bottom, top):
    domain_extent = padded_fields.shape[1]
    lowest_row = padded_fields[:, border_margin : border_margin + 1]
    highest_row = padded_fields[
        :, domain_extent - border_margin - 1 : domain_extent - border_margin
    ]
    plane_iota = lax.broadcasted_iota(jnp.int32, (1, domain_extent, 1, 1), 1)
    padded_fields = jnp.where(
        jnp.logical_and(bottom, plane_iota < border_margin), lowest_row, padded_fields
    )
    return jnp.where(
        jnp.logical_and(top, plane_iota >= domain_extent - border_margin),
        highest_row,
        padded_fields,
    )


def move_down(field_arrays):
    return passed_along(field_arrays, "grow", -1)


def body(labels, seed_blend, potential, inflow_index, liquid_table):
    grid_planes = labels.shape[0]
    growth_index = lax.axis_index("grow")
    devices_grow = lax.axis_size("grow")
    total_planes = grid_planes * devices_grow
    field_arrays = initial(labels, seed_blend, potential)

    def thermal_profile(domain_block, border_margin, domain_extent):
        plane = (
            domain_block * grid_planes
            - border_margin
            + lax.broadcasted_iota(jnp.int32, (domain_extent,), 0)
        )
        plane = plane.astype(jnp.float32)
        return (2.0 * (plane + 0.5) / float(total_planes) - 1.0)[:, None, None]

    lower_boundary = growth_index == 0
    upper_boundary = growth_index == devices_grow - 1
    padded_fields = with_halo(field_arrays, (("grow", 1), ("lat", 2)), 2)
    padded_fields = fix_ends(padded_fields, 2, lower_boundary, upper_boundary)
    halfway = evolve_fields(padded_fields, thermal_profile(growth_index, 1, grid_planes + 2))
    halfway = fix_ends(halfway, 1, lower_boundary, upper_boundary)
    result = move_down(evolve_fields(halfway, thermal_profile(growth_index, 0, grid_planes)))
    entering = inflow_fields(inflow_index, liquid_table)
    result = jnp.where(upper_boundary, entering, result)
    return (result[:4], result[4:])


def solution(mesh):
    in_specs = (
        P("grow", "lat", None),
        P(None, "grow", "lat", None),
        P(None, "grow", "lat", None),
        P(None, "lat", None),
        P(),
    )
    out_specs = (P(None, "grow", "lat", None), P(None, "grow", "lat", None))
    return jax.shard_map(body, mesh=mesh, in_specs=in_specs, out_specs=out_specs, check_vma=False)
```

profile of v0, /device:TPU:61, one launch (start us, length us, event | category | flops | bytes accessed | tf_op | source)
XLA Modules:
  0.0 92.6 jit_solution(5535426971800523772)
XLA Ops:
  0.6 1.4 %reduce_sum.113 = f32[8,32,256]{2,1,0:T(8,128)S(1)} reduce(f32[4,8,32,256]{3,2,1,0:T(8,128)} %param.10, f32[]{:T(128)} %constant.27.clone.1), dimensions={0}, to_apply=%region_2.3 | reduce | flops 196608 | bytes 1310724 | tf_op jit(solution)/shard_map/reduce_sum | solution.py:71
  2.4 0.7 copy-done
  3.2 3.2 %collective-permute-start = (f32[6,2,32,256]{3,2,0,1:T(8,128)S(1)}, f32[6,2,32,256]{3,2,0,1:T(8,128)S(1)}, u32[]{:S(2)}, u32[]{:S(2)}) collective-permute-start(f32[6,2,32,256]{3,2,0,1:T(8,128)S(1)} %get-tuple-element.44), channel_id=1, source_target_pairs={{0,8},{8,16},{16,24},{24,32},{32,40},{40,48},{48,56},{56,64},{64,7... | collective-permute-start | bytes 1179656 | tf_op jit(solution)/shard_map/ppermute | solution.py:25
  6.4 2.1 %collective-permute-start.1 = (f32[6,2,32,256]{3,2,0,1:T(8,128)S(1)}, f32[6,2,32,256]{3,2,0,1:T(8,128)S(1)}, u32[]{:S(2)}, u32[]{:S(2)}) collective-permute-start(f32[6,2,32,256]{3,2,0,1:T(8,128)S(1)} %get-tuple-element.45), channel_id=1, source_target_pairs={{8,0},{16,8},{24,16},{32,24},{40,32},{48,40},{56,48},{64,56},{72,6... | collective-permute-start | bytes 1179656 | tf_op jit(solution)/shard_map/ppermute | solution.py:26
  8.7 6.4 %collective-permute-done = f32[6,2,32,256]{3,2,0,1:T(8,128)S(1)} collective-permute-done((f32[6,2,32,256]{3,2,0,1:T(8,128)S(1)}, f32[6,2,32,256]{3,2,0,1:T(8,128)S(1)}, u32[]{:S(2)}, u32[]{:S(2)}) %collective-permute-start) | collective-permute-done | bytes 393248 | tf_op jit(solution)/shard_map/ppermute | solution.py:25
  15.1 5.0 %collective-permute-done.1 = f32[6,2,32,256]{3,2,0,1:T(8,128)S(1)} collective-permute-done((f32[6,2,32,256]{3,2,0,1:T(8,128)S(1)}, f32[6,2,32,256]{3,2,0,1:T(8,128)S(1)}, u32[]{:S(2)}, u32[]{:S(2)}) %collective-permute-start.1) | collective-permute-done | bytes 393248 | tf_op jit(solution)/shard_map/ppermute | solution.py:26
  20.3 7.6 %collective-permute-start.2 = (f32[6,12,2,256]{3,1,2,0:T(8,128)S(1)}, f32[6,12,2,256]{3,1,2,0:T(8,128)S(1)}, u32[]{:S(2)}, u32[]{:S(2)}) collective-permute-start(f32[6,12,2,256]{3,1,2,0:T(8,128)S(1)} %copy.28), channel_id=1, source_target_pairs={{0,1},{1,2},{2,3},{3,4},{4,5},{5,6},{6,7},{7,0},{8,9},{9,10},{10,1... | collective-permute-start | bytes 442376 | tf_op jit(solution)/shard_map/ppermute | solution.py:25
  27.9 1.9 %collective-permute-start.3 = (f32[6,12,2,256]{3,1,2,0:T(8,128)S(1)}, f32[6,12,2,256]{3,1,2,0:T(8,128)S(1)}, u32[]{:S(2)}, u32[]{:S(2)}) collective-permute-start(f32[6,12,2,256]{3,1,2,0:T(8,128)S(1)} %copy.29), channel_id=1, source_target_pairs={{1,0},{2,1},{3,2},{4,3},{5,4},{6,5},{7,6},{0,7},{9,8},{10,9},{11,1... | collective-permute-start | bytes 442376 | tf_op jit(solution)/shard_map/ppermute | solution.py:26
  29.8 0.6 collective-permute-done.2
  30.5 7.4 %collective-permute-done.3 = f32[6,12,2,256]{3,1,2,0:T(8,128)S(1)} collective-permute-done((f32[6,12,2,256]{3,1,2,0:T(8,128)S(1)}, f32[6,12,2,256]{3,1,2,0:T(8,128)S(1)}, u32[]{:S(2)}, u32[]{:S(2)}) %collective-permute-start.3) | collective-permute-done | bytes 147488 | tf_op jit(solution)/shard_map/ppermute | solution.py:26
  38.6 0.9 select_select_fusion
  39.5 0.9 %fusion.46 = (f32[6,10,34,255]{3,2,0,1:T(8,128)S(1)}, f32[6,10,34,255]{3,2,0,1:T(8,128)S(1)}) fusion(f32[6,12,36,256]{3,2,0,1:T(8,128)S(1)} %select_select_fusion), kind=kLoop, calls=%fused_computation.117 | loop fusion | bytes 8323200 | tf_op jit(solution)/shard_map/jit(_roll_static)/slice | solution.py:38
  41.0 2.1 %fusion = f32[6,10,34,256]{3,2,0,1:T(8,128)S(1)} fusion(f32[6,12,36,256]{3,2,0,1:T(8,128)S(1)} %select_select_fusion, f32[6,10,34,1]{3,2,0,1:T(8,128)S(1)} %get-tuple-element.29, f32[6,10,34,255]{3,2,0,1:T(8,128)S(1)} %get-tuple-element.31, f32[6,10,34,255]{3,2,0,1:T(8,128)S(1)} %get-tuple-element.30, f32[6,10,34,1]{3,2,0,1:T(8,128)S(1)} %get-tuple-element.28), kind=kLoop, calls=%fused_computation.6 | loop fusion | flops 4700160 | bytes 16711680 | tf_op jit(solution)/shard_map/sub | solution.py:38
  43.1 1.1 %fusion.43 = (f32[10,34,256]{2,1,0:T(8,128)S(1)}, f32[4,10,34,256]{3,2,0,1:T(8,128)S(1)}) fusion(f32[4,10]{0,1:T(8,128)S(1)} %broadcast_multiply_fusion.2, f32[4]{0:T(128)S(1)} %copy-done.5, f32[10,34,256]{2,1,0:T(8,128)S(1)} %get-tuple-element.26, f32[4]{0:T(128)S(1)} %copy-done.4, f32[10,34,256]{2,1,0:T(8,128)S(1)} %get-tuple-element.27, ...), kind=kLoop, calls=%fused_computation.115 | loop fusion | flops 5483520 | bytes 5222592 | tf_op jit(solution)/shard_map/reduce_sum | solution.py:53
  44.2 1.0 %fusion.8 = (f32[10,34,256]{2,1,0:T(8,128)S(1)}, f32[10,34,256]{2,1,0:T(8,128)S(1)}, f32[10,34,256]{2,1,0:T(8,128)S(1)}, f32[4,10,34,256]{3,2,0,1:T(8,128)S(1)}) fusion(f32[4]{0:T(128)S(1)} %copy-done.4, f32[10,34,256]{2,1,0:T(8,128)S(1)} %get-tuple-element.27, f32[6,12,36,256]{3,2,0,1:T(8,128)S(1)} %select_select_fusion, f32[4]{0:T(128)S(1)} %copy-done.5, ...), kind=kLoop, calls=%fused_computation.24 | loop fusion | flops 4264960 | bytes 6266912 | tf_op jit(solution)/shard_map/reduce_sum | solution.py:61
  46.3 0.7 fusion.48
  47.3 0.9 fusion.12
  48.2 0.7 fusion.41
  49.0 0.6 fusion.20
  49.9 1.9 %collective-permute-start.4 = (f32[6,8,32,256]{3,2,0,1:T(8,128)S(1)}, f32[6,8,32,256]{3,2,0,1:T(8,128)S(1)}, u32[]{:S(2)}, u32[]{:S(2)}) collective-permute-start(f32[6,8,32,256]{3,2,0,1:T(8,128)S(1)} %pad_maximum_fusion.2), channel_id=1, source_target_pairs={{8,0},{16,8},{24,16},{32,24},{40,32},{48,40},{56,48},{64,56},{72,6... | collective-permute-start | bytes 4718600 | tf_op jit(solution)/shard_map/ppermute | solution.py:15
  52.0 0.7 select_reduce_fusion
  52.8 37.4 %collective-permute-done.4 = f32[6,8,32,256]{3,2,0,1:T(8,128)S(1)} collective-permute-done((f32[6,8,32,256]{3,2,0,1:T(8,128)S(1)}, f32[6,8,32,256]{3,2,0,1:T(8,128)S(1)}, u32[]{:S(2)}, u32[]{:S(2)}) %collective-permute-start.4) | collective-permute-done | bytes 1572896 | tf_op jit(solution)/shard_map/ppermute | solution.py:15
  90.7 1.1 %copy.32 = f32[4,8,32,256]{3,2,1,0:T(8,128)} copy(f32[4,8,32,256]{3,2,0,1:T(8,128)S(1)} %slice.268) | data formatting | bytes 2097152
  91.8 0.8 copy.33
  (52 shorter events, 4.3 us)
Async XLA Ops:
  0.6 1.5 %copy-start.1 = (f32[4,8,32,256]{3,2,1,0:T(8,128)S(1)}, f32[4,8,32,256]{3,2,1,0:T(8,128)}, u32[]{:S(2)}) copy-start(f32[4,8,32,256]{3,2,1,0:T(8,128)} %param.10) | copy-start | bytes 3145732
  0.6 1.6 %copy-start.2 = (s32[8,32,256]{2,1,0:T(8,128)S(1)}, s32[8,32,256]{2,1,0:T(8,128)}, u32[]{:S(2)}) copy-start(s32[8,32,256]{2,1,0:T(8,128)} %param.9) | copy-start | bytes 786436
  2.1 1.1 %copy-start = (f32[2,8,32,256]{3,2,1,0:T(8,128)S(1)}, f32[2,8,32,256]{3,2,1,0:T(8,128)}, u32[]{:S(2)}) copy-start(f32[2,8,32,256]{3,2,1,0:T(8,128)} %param.11) | copy-start | bytes 1572868
  3.2 5.4 %copy-start.6 = (f32[4]{0:T(128)S(1)}, f32[4]{0:T(128)}, u32[]{:S(2)}) copy-start(f32[4]{0:T(128)} %constant.19.clone) | copy-start | bytes 52
  3.2 11.9 %collective-permute-start = (f32[6,2,32,256]{3,2,0,1:T(8,128)S(1)}, f32[6,2,32,256]{3,2,0,1:T(8,128)S(1)}, u32[]{:S(2)}, u32[]{:S(2)}) collective-permute-start(f32[6,2,32,256]{3,2,0,1:T(8,128)S(1)} %get-tuple-element.44), channel_id=1, source_target_pairs={{0,8},{8,16},{16,24},{24,32},{32,40},{40,48},{48,56},{56,64},{64,7... | collective-permute-start | bytes 1179656 | tf_op jit(solution)/shard_map/ppermute | solution.py:25
  6.4 13.7 %collective-permute-start.1 = (f32[6,2,32,256]{3,2,0,1:T(8,128)S(1)}, f32[6,2,32,256]{3,2,0,1:T(8,128)S(1)}, u32[]{:S(2)}, u32[]{:S(2)}) collective-permute-start(f32[6,2,32,256]{3,2,0,1:T(8,128)S(1)} %get-tuple-element.45), channel_id=1, source_target_pairs={{8,0},{16,8},{24,16},{32,24},{40,32},{48,40},{56,48},{64,56},{72,6... | collective-permute-start | bytes 1179656 | tf_op jit(solution)/shard_map/ppermute | solution.py:26
  20.3 10.2 %collective-permute-start.2 = (f32[6,12,2,256]{3,1,2,0:T(8,128)S(1)}, f32[6,12,2,256]{3,1,2,0:T(8,128)S(1)}, u32[]{:S(2)}, u32[]{:S(2)}) collective-permute-start(f32[6,12,2,256]{3,1,2,0:T(8,128)S(1)} %copy.28), channel_id=1, source_target_pairs={{0,1},{1,2},{2,3},{3,4},{4,5},{5,6},{6,7},{7,0},{8,9},{9,10},{10,1... | collective-permute-start | bytes 442376 | tf_op jit(solution)/shard_map/ppermute | solution.py:25
  27.9 10.1 %collective-permute-start.3 = (f32[6,12,2,256]{3,1,2,0:T(8,128)S(1)}, f32[6,12,2,256]{3,1,2,0:T(8,128)S(1)}, u32[]{:S(2)}, u32[]{:S(2)}) collective-permute-start(f32[6,12,2,256]{3,1,2,0:T(8,128)S(1)} %copy.29), channel_id=1, source_target_pairs={{1,0},{2,1},{3,2},{4,3},{5,4},{6,5},{7,6},{0,7},{9,8},{10,9},{11,1... | collective-permute-start | bytes 442376 | tf_op jit(solution)/shard_map/ppermute | solution.py:26
  41.0 2.1 %copy-start.4 = (f32[4]{0:T(128)S(1)}, f32[4]{0:T(128)}, u32[]{:S(2)}) copy-start(f32[4]{0:T(128)} %constant.83) | copy-start | bytes 52
  41.0 2.1 %copy-start.5 = (f32[4]{0:T(128)S(1)}, f32[4]{0:T(128)}, u32[]{:S(2)}) copy-start(f32[4]{0:T(128)} %constant.85) | copy-start | bytes 52
  49.7 2.2 %copy-start.7 = (f32[16,2]{0,1:T(2,128)S(1)}, f32[16,2]{0,1:T(2,128)}, u32[]{:S(2)}) copy-start(f32[16,2]{0,1:T(2,128)} %param.13) | copy-start | bytes 388
  49.8 2.2 %copy-start.3 = (s32[8,32,256]{2,1,0:T(8,128)S(1)}, s32[8,32,256]{2,1,0:T(8,128)}, u32[]{:S(2)}) copy-start(s32[8,32,256]{2,1,0:T(8,128)} %param.12) | copy-start | bytes 786436
  49.9 40.3 %collective-permute-start.4 = (f32[6,8,32,256]{3,2,0,1:T(8,128)S(1)}, f32[6,8,32,256]{3,2,0,1:T(8,128)S(1)}, u32[]{:S(2)}, u32[]{:S(2)}) collective-permute-start(f32[6,8,32,256]{3,2,0,1:T(8,128)S(1)} %pad_maximum_fusion.2), channel_id=1, source_target_pairs={{8,0},{16,8},{24,16},{32,24},{40,32},{48,40},{56,48},{64,56},{72,6... | collective-permute-start | bytes 4718600 | tf_op jit(solution)/shard_map/ppermute | solution.py:15
where the time goes:
time: 92.9 us; the launch traced here: 92.6 us
  waiting for transfers between devices  56.8 us (61%)
  starting transfers between devices  16.7 us (18%)
  other arithmetic  12.2 us (13%)
  local copies, waits for them, and re-layouts  5.87 us (6%)
  between operations  1.1 us (1%)
    ppermute x1, waiting for transfers between devices, passed_along(): return lax.ppermute(block, axis, route)  37.4 us
    ppermute x2, waiting for transfers between devices, with_halo(): after = lax.ppermute(first, axis, down)  12.4 us
    ppermute x2, starting transfers between devices, with_halo(): before = lax.ppermute(last, axis, up)  10.8 us
    ppermute x2, waiting for transfers between devices, with_halo(): before = lax.ppermute(last, axis, up)  6.98 us
    ppermute x2, starting transfers between devices, with_halo(): after = lax.ppermute(first, axis, down)  4 us
    sub x2, other arithmetic, evolve_fields(): laplace + (jnp.roll(centre, -1, axis=3) + jnp.roll(centre, 1, axis=3))  2.99 us
    unnamed x22, local copies, waits for them, and re-layouts  2.88 us
    slice x4, local copies, waits for them, and re-layouts, evolve_fields(): jnp.roll(centre, 1, axis=3)  2.37 us
  transfers between devices with their start and end apart: 5, of which 5 were waited for; matrix products, arithmetic and copies ran while one was open for 1% of the time, Pallas kernels for 0%

commit v1 on v0

v1 whole, which is shorter than its diff:
```python
import functools

import jax
import jax.numpy as jnp
from jax import lax
from jax.experimental import pallas as pl
from jax.experimental.pallas import tpu as pltpu
from jax.sharding import PartitionSpec as P

offset_table = ((0.0, 0.0), (0.6, -0.3), (-0.4, 0.5), (-0.2, -0.6))
latent_heat = (0.0, 0.8, 0.8, 0.8)
relax_rate = 0.1
diffusion = 0.05

shift = 2
fields = 5
tile = 8

VMEM = pl.BlockSpec(memory_space=pltpu.VMEM)
SMEM = pl.BlockSpec(memory_space=pltpu.SMEM)
ANY = pl.BlockSpec(memory_space=pl.ANY)


def step_tile(below, above, centre, before, after, temp):
    row = lax.broadcasted_iota(jnp.int32, centre[0].shape, 0)
    last = centre[0].shape[0] - 1
    width = centre[0].shape[1]
    laps = []
    for f in range(fields):
        c = centre[f]
        x_minus = pltpu.roll(jnp.where(row == last, before[f], c), 1, 0)
        x_plus = pltpu.roll(jnp.where(row == 0, after[f], c), last, 0)
        y_minus = pltpu.roll(c, 1, 1)
        y_plus = pltpu.roll(c, width - 1, 1)
        laps.append(
            (above[f] + below[f]) + (x_plus + x_minus) + (y_plus + y_minus) - 6.0 * c
        )
    p = list(centre[:3])
    p.append(1.0 - (p[0] + p[1] + p[2]))
    mu = centre[3:]
    common = 1.0 - (mu[0] * mu[0] + mu[1] * mu[1])
    react = []
    for a in range(4):
        e0, e1 = offset_table[a]
        w = common
        if a:
            w = w - (2.0 * e0) * mu[0] - (2.0 * e1) * mu[1]
            w = w + (2.0 * latent_heat[a] * temp - (e0 * e0 + e1 * e1))
        react.append(p[a] * (w + p[a] * (2.0 * p[a] - 3.0)))
    mean = 0.25 * ((react[0] + react[1]) + (react[2] + react[3]))
    new = [p[a] + relax_rate * (laps[a] + (mean - react[a])) for a in range(3)]
    new.append(1.0 - (new[0] + new[1] + new[2]))
    squares = [n * n for n in new]
    growth = [squares[a] - p[a] * p[a] for a in range(4)]
    sus = (squares[0] + squares[1]) + (squares[2] + squares[3])
    grown = (growth[0] + growth[1]) + (growth[2] + growth[3])
    mobile = diffusion * 0.1 + diffusion * squares[0]
    inverse = 1.0 / sus
    out = new[:3]
    for k in range(2):
        source = mu[k] * grown
        for a in range(1, 4):
            source = source + offset_table[a][k] * growth[a]
        out.append(mu[k] + (mobile * laps[3 + k] - source) * inverse)
    return out


def step_plane(src, at, dst, to, temp, tiles, all_tiles):
    for t in range(tiles):
        def rows(plane, u):
            u = (u + all_tiles) % all_tiles
            return [src[plane, f, u * tile : (u + 1) * tile, :] for f in range(fields)]

        new = step_tile(
            rows(at - 1, t), rows(at + 1, t), rows(at, t), rows(at, t - 1), rows(at, t + 1), temp
        )
        for f in range(fields):
            dst[to, f, t * tile : (t + 1) * tile, :] = new[f]


def start_kernel(labels, seed, potential, state, state_send, first_rows, last_rows):
    planes, height = labels.shape[0], labels.shape[1]
    for z in range(planes):
        total = 1.0 + ((seed[0, z] + seed[1, z]) + (seed[2, z] + seed[3, z]))
        scale = 1.0 / total
        lab = labels[z]
        vals = [(jnp.where(lab == a, 1.0, 0.0) + seed[a, z]) * scale for a in range(3)]
        vals += [potential[0, z], potential[1, z]]
        for f in range(fields):
            state[z, f] = vals[f]
            if z < shift + 2:
                state_send[z, f] = vals[f]
            at = 2 * (z * fields + f)
            first_rows[at : at + 2, :] = vals[f][0:2, :]
            last_rows[at : at + 2, :] = vals[f][height - 2 : height, :]


def gather_planes(dst, places, height):
    for i, (main, z, after, before, w) in enumerate(places):
        for f in range(fields):
            dst[i, f, 0:height, :] = main[z, f]
            at = 2 * (w * fields + f)
            dst[i, f, height : height + 2, :] = after[at : at + 2, :]
            dst[i, f, height + 6 : height + 8, :] = before[at : at + 2, :]


def temp_of(place, z, total):
    plane = (place + z).astype(jnp.float32)
    return 2.0 * (plane + 0.5) / float(total) - 1.0


def own_kernel(total, place, state, after, before, done, carry, padded, half):
    planes, height = state.shape[0], state.shape[2]
    tiles = height // tile
    first = shift - 2
    gather_planes(
        padded, [(state, z, after, before, z) for z in range(first, planes)], height
    )
    base = place[0]

    def one(i, _):
        step_plane(padded, i + 1, half, i, temp_of(base, i + first + 1, total), tiles + 1, tiles + 1)
        return 0

    n = planes - first
    lax.fori_loop(0, n - 2, one, 0)

    def two(i, _):
        step_plane(half, i + 1, done, i, temp_of(base, i + shift, total), tiles, tiles + 1)
        return 0

    lax.fori_loop(0, n - 4, two, 0)
    carry[...] = half[n - 4 : n - 2]


def edge_kernel(total, place, state, after, before, upper, upper_after, upper_before, carry,
                done, carry_out, padded, half):
    planes, height = state.shape[0], state.shape[2]
    tiles = height // tile
    base = place[0]
    top = base == total - planes
    gather_planes(
        padded,
        [(state, planes - 2, after, before, planes - 2), (state, planes - 1, after, before, planes - 1)]
        + [(upper, z, upper_after, upper_before, z) for z in range(2)],
        height,
    )

    @pl.when(top)
    def _():
        padded[2] = padded[1]

    half[0:2] = carry[...]

    def one(i, _):
        step_plane(padded, i + 1, half, i + 2, temp_of(base, i + planes - 1, total), tiles + 1, tiles + 1)
        return 0

    lax.fori_loop(0, 2, one, 0)

    @pl.when(top)
    def _():
        half[3] = half[2]

    def two(i, _):
        step_plane(half, i + 1, done, i, temp_of(base, i + planes - 2, total), tiles, tiles + 1)
        return 0

    lax.fori_loop(0, 2, two, 0)
    carry_out[...] = half[2:4]


def upper_kernel(total, place, upper, upper_after, upper_before, carry, done, padded, half):
    height = upper.shape[2]
    tiles = height // tile
    base = place[0]
    planes = place[1]
    gather_planes(padded, [(upper, z, upper_after, upper_before, z) for z in range(shift + 2)], height)
    half[0:2] = carry[...]

    def one(i, _):
        step_plane(padded, i + 1, half, i + 2, temp_of(base + planes, i + 1, total), tiles + 1, tiles + 1)
        return 0

    lax.fori_loop(0, shift, one, 0)

    def two(i, _):
        step_plane(half, i + 1, done, i, temp_of(base + planes, i, total), tiles, tiles + 1)
        return 0

    lax.fori_loop(0, shift, two, 0)


def finish_kernel(total, liquids, place, table, low, middle, high, inflow, phase, chem, extra, sems):
    planes = phase.shape[1]
    parts = [(low, 0, shift), (middle, shift, planes - 2), (high, planes - 2, planes)]
    top = place[0] == total - planes

    @pl.when(jnp.logical_not(top))
    def _():
        copies = []
        for part, first, end in parts:
            for f in range(fields):
                if f < 3:
                    dst = phase.at[f, pl.ds(first, end - first)]
                else:
                    dst = chem.at[f - 3, pl.ds(first, end - first)]
                copy = pltpu.make_async_copy(part.at[:, f], dst, sems.at[len(copies)])
                copy.start()
                copies.append(copy)
        for part, first, end in parts:
            for z in range(first, end):
                extra[0, z] = 1.0 - (part[z - first, 0] + part[z - first, 1] + part[z - first, 2])
        copy = pltpu.make_async_copy(extra.at[0], phase.at[3], sems.at[len(copies)])
        copy.start()
        copies.append(copy)
        for copy in copies:
            copy.wait()

    @pl.when(top)
    def _():
        extra[0] = jnp.ones(extra.shape[1:], jnp.float32)
        extra[1] = jnp.zeros(extra.shape[1:], jnp.float32)

        def lookup(z, _):
            kind = inflow[z]
            for k in range(2):
                value = jnp.zeros(kind.shape, jnp.float32)
                for j in range(liquids):
                    value = jnp.where(kind == j, table[j, k], value)
                extra[2 + k, z] = value
            return 0

        lax.fori_loop(0, planes, lookup, 0)
        copies = []
        pairs = [(0, phase.at[0]), (1, phase.at[1]), (1, phase.at[2]), (1, phase.at[3]),
                 (2, chem.at[0]), (3, chem.at[1])]
        for i, (j, dst) in enumerate(pairs):
            copy = pltpu.make_async_copy(extra.at[j], dst, sems.at[i])
            copy.start()
            copies.append(copy)
        for copy in copies:
            copy.wait()


def f32(*shape):
    return jax.ShapeDtypeStruct(shape, jnp.float32)


def ring(block, axis, distance):
    count = lax.axis_size(axis)
    return lax.ppermute(block, axis, [(i, (i + distance) % count) for i in range(count)])


def body(labels, seed_blend, potential, inflow_index, liquid_table):
    planes, height, width = labels.shape
    total = planes * lax.axis_size("grow")
    base = lax.axis_index("grow") * planes
    place = jnp.stack([base, jnp.int32(planes)]).astype(jnp.int32)
    padded_rows = height + tile
    params = pltpu.CompilerParams(vmem_limit_bytes=24 * 1024 * 1024)

    def call(kernel, out_shape, in_specs, scratch=(), out_specs=None):
        return pl.pallas_call(
            kernel,
            out_shape=out_shape,
            in_specs=in_specs,
            out_specs=out_specs if out_specs is not None else jax.tree.map(lambda _: VMEM, out_shape),
            scratch_shapes=list(scratch),
            compiler_params=params,
        )

    state, send, first_rows, last_rows = call(
        start_kernel,
        (
            f32(planes, fields, height, width),
            f32(shift + 2, fields, height, width),
            f32(2 * planes * fields, width),
            f32(2 * planes * fields, width),
        ),
        [VMEM] * 3,
    )(labels, seed_blend, potential)

    upper = ring(send, "grow", -1)
    after = ring(first_rows, "lat", -1)
    before = ring(last_rows, "lat", 1)

    middle, carry = call(
        functools.partial(own_kernel, total),
        (f32(planes - 2 - shift, fields, height, width), f32(2, fields, padded_rows, width)),
        [SMEM] + [VMEM] * 3,
        [
            pltpu.VMEM((planes - shift + 2, fields, padded_rows, width), jnp.float32),
            pltpu.VMEM((planes - shift, fields, padded_rows, width), jnp.float32),
        ],
    )(place, state, after, before)
    middle_got = ring(middle, "grow", -1)

    rows = (shift + 2) * fields * 2
    upper_first = upper[:, :, 0:2].reshape(rows, width)
    upper_last = upper[:, :, height - 2 : height].reshape(rows, width)
    upper_after = ring(upper_first, "lat", -1)
    upper_before = ring(upper_last, "lat", 1)

    high, carry = call(
        functools.partial(edge_kernel, total),
        (f32(2, fields, height, width), f32(2, fields, padded_rows, width)),
        [SMEM] + [VMEM] * 7,
        [
            pltpu.VMEM((4, fields, padded_rows, width), jnp.float32),
            pltpu.VMEM((4, fields, padded_rows, width), jnp.float32),
        ],
    )(place, state, after, before, upper, upper_after, upper_before, carry)
    high_got = ring(high, "grow", -1)

    low = call(
        functools.partial(upper_kernel, total),
        f32(shift, fields, height, width),
        [SMEM] + [VMEM] * 4,
        [
            pltpu.VMEM((shift + 2, fields, padded_rows, width), jnp.float32),
            pltpu.VMEM((shift + 2, fields, padded_rows, width), jnp.float32),
        ],
    )(place, upper, upper_after, upper_before, carry)

    return call(
        functools.partial(finish_kernel, total, liquid_table.shape[0]),
        (f32(4, planes, height, width), f32(2, planes, height, width)),
        [SMEM, SMEM] + [VMEM] * 4,
        [pltpu.VMEM((4, planes, height, width), jnp.float32), pltpu.SemaphoreType.DMA((3 * fields + 1,))],
        (ANY, ANY),
    )(place, liquid_table, low, middle_got, high_got, inflow_index)


def solution(mesh):
    in_specs = (
        P("grow", "lat", None),
        P(None, "grow", "lat", None),
        P(None, "grow", "lat", None),
        P(None, "lat", None),
        P(),
    )
    out_specs = (P(None, "grow", "lat", None), P(None, "grow", "lat", None))
    return jax.shard_map(body, mesh=mesh, in_specs=in_specs, out_specs=out_specs, check_vma=False)
```

time: 92.9 us -> 76.3 us (0.82)
  the two profiles are of different devices: /device:TPU:61 before, /device:TPU:1 now
where the time goes in v1:
time: 76.3 us; the launch traced here: 75.6 us
  starting transfers between devices  51.4 us (67%)
  Pallas kernels  10.4 us (14%)
  local copies, waits for them, and re-layouts  7.25 us (10%)
  waiting for transfers between devices  5.78 us (8%)
  between operations  0.78 us (1%)
    ppermute x7, starting transfers between devices, ring(): lax.ppermute(block, axis, [(i, (i + distance) % count) for i in range(cou...  51.4 us
    unnamed x25, local copies, waits for them, and re-layouts  7.15 us
    ppermute x7, waiting for transfers between devices, ring(): lax.ppermute(block, axis, [(i, (i + distance) % count) for i in range(cou...  5.78 us
    pallas_call x1, Pallas kernels, body(): call(functools.partial(own_kernel, total), (f32(planes - 2 - shift, field...  3.73 us
    pallas_call x1, Pallas kernels, body(): call(functools.partial(edge_kernel, total), (f32(2, fields, height, width...  2.22 us
    pallas_call x1, Pallas kernels, body(): call(functools.partial(finish_kernel, total, liquid_table.shape[0]), (f32...  1.94 us
  transfers between devices with their start and end apart: 7, of which 4 were waited for; matrix products, arithmetic and copies ran while one was open for 0% of the time, Pallas kernels for 10%

profile of v1, /device:TPU:1, one launch (start us, length us, event | category | flops | bytes accessed | tf_op | source)
XLA Modules:
  0.0 75.6 jit_solution(16756493224241475242)
XLA Ops:
  0.6 1.2 %copy-done = f32[4,8,32,256]{3,2,1,0:T(8,128)S(1)} copy-done((f32[4,8,32,256]{3,2,1,0:T(8,128)S(1)}, f32[4,8,32,256]{3,2,1,0:T(8,128)}, u32[]{:S(2)}) %copy-start) | copy-done | bytes 1048600
  1.9 1.0 %copy-done.1 = f32[2,8,32,256]{3,2,1,0:T(8,128)S(1)} copy-done((f32[2,8,32,256]{3,2,1,0:T(8,128)S(1)}, f32[2,8,32,256]{3,2,1,0:T(8,128)}, u32[]{:S(2)}) %copy-start.1) | copy-done | bytes 524312
  2.9 0.9 %copy-done.4 = s32[8,32,256]{2,1,0:T(8,128)S(1)} copy-done((s32[8,32,256]{2,1,0:T(8,128)S(1)}, s32[8,32,256]{2,1,0:T(8,128)}, u32[]{:S(2)}) %copy-start.4) | copy-done | bytes 262168
  3.8 1.0 %shard_map.68 = (f32[8,5,32,256]{3,2,1,0:T(8,128)S(1)}, f32[4,5,32,256]{3,2,1,0:T(8,128)}, f32[80,256]{1,0:T(8,128)S(1)}, f32[80,256]{1,0:T(8,128)S(1)}) custom-call(s32[8,32,256]{2,1,0:T(8,128)S(1)} %copy-done.4, f32[4,8,32,256]{3,2,1,0:T(8,128)S(1)} %copy-done, f32[2,8,32,256]{3,2,1,0:T(8,128)S(1)} %copy-done.1), custom_call_target="tpu_custom_call" | custom-call | tf_op jit(solution)/shard_map/pallas_call | solution.py:273
  4.8 9.9 %collective-permute-start = (f32[4,5,32,256]{3,2,1,0:T(8,128)}, f32[4,5,32,256]{3,2,1,0:T(8,128)S(1)}, u32[]{:S(2)}, u32[]{:S(2)}) collective-permute-start(f32[4,5,32,256]{3,2,1,0:T(8,128)} %get-tuple-element.10), channel_id=1, source_target_pairs={{0,504},{8,0},{16,8},{24,16},{32,24},{40,32},{48,40},{56,48},{64,5... | collective-permute-start | bytes 1966088 | tf_op jit(solution)/shard_map/ppermute | solution.py:252
  14.7 2.9 %collective-permute-start.3 = (f32[80,256]{1,0:T(8,128)S(1)}, f32[80,256]{1,0:T(8,128)S(1)}, u32[]{:S(2)}, u32[]{:S(2)}) collective-permute-start(f32[80,256]{1,0:T(8,128)S(1)} %get-tuple-element.12), channel_id=1, source_target_pairs={{0,7},{1,0},{2,1},{3,2},{4,3},{5,4},{6,5},{7,6},{8,15},{9,8},{10,9... | collective-permute-start | bytes 245768 | tf_op jit(solution)/shard_map/ppermute | solution.py:252
  17.6 5.7 %collective-permute-start.4 = (f32[80,256]{1,0:T(8,128)S(1)}, f32[80,256]{1,0:T(8,128)S(1)}, u32[]{:S(2)}, u32[]{:S(2)}) collective-permute-start(f32[80,256]{1,0:T(8,128)S(1)} %get-tuple-element.13), channel_id=1, source_target_pairs={{0,1},{1,2},{2,3},{3,4},{4,5},{5,6},{6,7},{7,0},{8,9},{9,10},{10,1... | collective-permute-start | bytes 245768 | tf_op jit(solution)/shard_map/ppermute | solution.py:252
  23.4 0.1 collective-permute-done.3.after
  23.5 4.1 %collective-permute-done.4.before = f32[80,256]{1,0:T(8,128)S(1)} collective-permute-done((f32[80,256]{1,0:T(8,128)S(1)}, f32[80,256]{1,0:T(8,128)S(1)}, u32[]{:S(2)}, u32[]{:S(2)}) %collective-permute-start.4) | collective-permute-done | bytes 81952 | tf_op jit(solution)/shard_map/ppermute | solution.py:252
  27.6 3.7 %shard_map.69 = (f32[4,5,32,256]{3,2,1,0:T(8,128)}, f32[2,5,40,256]{3,2,1,0:T(8,128)S(1)}) custom-call(s32[2]{0:T(128)S(1)} %pad_add_fusion.place, f32[8,5,32,256]{3,2,1,0:T(8,128)S(1)} %get-tuple-element.11.state, f32[80,256]{1,0:T(8,128)S(1)} %collective-permute-done.3.after, f32[80,256]{1,0:T(8,128)S(1)} %collective-permute-done.4.before), custom_call_target="tpu_custom_call" | custom-call | tf_op jit(solution)/shard_map/pallas_call | solution.py:288
  31.3 11.4 %collective-permute-start.5 = (f32[4,5,32,256]{3,2,1,0:T(8,128)}, f32[4,5,32,256]{3,2,1,0:T(8,128)S(1)}, u32[]{:S(2)}, u32[]{:S(2)}) collective-permute-start(f32[4,5,32,256]{3,2,1,0:T(8,128)} %get-tuple-element.16), channel_id=1, source_target_pairs={{0,504},{8,0},{16,8},{24,16},{32,24},{40,32},{48,40},{56,48},{64,5... | collective-permute-start | bytes 1966088 | tf_op jit(solution)/shard_map/ppermute | solution.py:252
  42.8 1.9 %collective-permute-start.1 = (f32[40,256]{1,0:T(8,128)S(1)}, f32[40,256]{1,0:T(8,128)S(1)}, u32[]{:S(2)}, u32[]{:S(2)}) collective-permute-start(f32[40,256]{1,0:T(8,128)S(1)} %reshape.10), channel_id=1, source_target_pairs={{0,7},{1,0},{2,1},{3,2},{4,3},{5,4},{6,5},{7,6},{8,15},{9,8},{10,9... | collective-permute-start | bytes 122888 | tf_op jit(solution)/shard_map/ppermute | solution.py:252
  44.8 4.5 %collective-permute-start.2 = (f32[40,256]{1,0:T(8,128)S(1)}, f32[40,256]{1,0:T(8,128)S(1)}, u32[]{:S(2)}, u32[]{:S(2)}) collective-permute-start(f32[40,256]{1,0:T(8,128)S(1)} %reshape.11), channel_id=1, source_target_pairs={{0,1},{1,2},{2,3},{3,4},{4,5},{5,6},{6,7},{7,0},{8,9},{9,10},{10,1... | collective-permute-start | bytes 122888 | tf_op jit(solution)/shard_map/ppermute | solution.py:252
  49.3 0.6 copy-done.6
  49.9 0.4 collective-permute-done.2.upper_before
  50.4 0.9 %copy-done.3 = f32[80,256]{1,0:T(8,128)S(1)} copy-done((f32[80,256]{1,0:T(8,128)S(1)}, f32[80,256]{1,0:T(8,128)}, u32[]{:S(2)}) %copy-start.3) | copy-done | bytes 81944
  51.3 0.8 %copy-done.7 = f32[40,256]{1,0:T(8,128)S(1)} copy-done((f32[40,256]{1,0:T(8,128)S(1)}, f32[40,256]{1,0:T(8,128)}, u32[]{:S(2)}) %copy-start.7) | copy-done | bytes 40984
  52.1 2.2 %shard_map.70 = (f32[2,5,32,256]{3,2,1,0:T(8,128)}, f32[2,5,40,256]{3,2,1,0:T(8,128)S(1)}) custom-call(s32[2]{0:T(128)S(1)} %pad_add_fusion.place, f32[8,5,32,256]{3,2,1,0:T(8,128)S(1)} %get-tuple-element.11.state, f32[80,256]{1,0:T(8,128)S(1)} %collective-permute-done.3.after, f32[80,256]{1,0:T(8,128)S(1)} %copy-done.3, ...), custom_call_target="tpu_custom_call" | custom-call | tf_op jit(solution)/shard_map/pallas_call | solution.py:305
  54.3 15.1 %collective-permute-start.6 = (f32[2,5,32,256]{3,2,1,0:T(8,128)}, f32[2,5,32,256]{3,2,1,0:T(8,128)S(1)}, u32[]{:S(2)}, u32[]{:S(2)}) collective-permute-start(f32[2,5,32,256]{3,2,1,0:T(8,128)} %get-tuple-element.17), channel_id=1, source_target_pairs={{0,504},{8,0},{16,8},{24,16},{32,24},{40,32},{48,40},{56,48},{64,5... | collective-permute-start | bytes 983048 | tf_op jit(solution)/shard_map/ppermute | solution.py:252
  69.5 0.8 %copy-done.8 = f32[40,256]{1,0:T(8,128)S(1)} copy-done((f32[40,256]{1,0:T(8,128)S(1)}, f32[40,256]{1,0:T(8,128)}, u32[]{:S(2)}) %copy-start.8) | copy-done | bytes 40984
  70.3 0.8 %copy-done.10 = f32[40,256]{1,0:T(8,128)S(1)} copy-done((f32[40,256]{1,0:T(8,128)S(1)}, f32[40,256]{1,0:T(8,128)}, u32[]{:S(2)}) %copy-start.10) | copy-done | bytes 40984
  71.0 1.5 %shard_map.71.low = f32[2,5,32,256]{3,2,1,0:T(8,128)S(1)} custom-call(s32[2]{0:T(128)S(1)} %pad_add_fusion.place, f32[4,5,32,256]{3,2,1,0:T(8,128)S(1)} %collective-permute-done.upper, f32[40,256]{1,0:T(8,128)S(1)} %copy-done.8, f32[40,256]{1,0:T(8,128)S(1)} %copy-done.10, f32[2,5,40,256]{3,2,1,0:T(8,128)S(1)} %get-tuple-element.15.carry), custom_call_target="tpu_custom_call" | custom-call | tf_op jit(solution)/shard_map/pallas_call | solution.py:316
  72.5 1.2 %collective-permute-done.6.high = f32[2,5,32,256]{3,2,1,0:T(8,128)S(1)} collective-permute-done((f32[2,5,32,256]{3,2,1,0:T(8,128)}, f32[2,5,32,256]{3,2,1,0:T(8,128)S(1)}, u32[]{:S(2)}, u32[]{:S(2)}) %collective-permute-start.6) | collective-permute-done | bytes 327712 | tf_op jit(solution)/shard_map/ppermute | solution.py:252
  73.7 1.9 %shard_map.72 = (f32[4,8,32,256]{3,2,1,0:T(8,128)}, f32[2,8,32,256]{3,2,1,0:T(8,128)}) custom-call(s32[2]{0:T(128)S(1)} %pad_add_fusion.place, f32[16,2]{1,0:T(8,128)S(1)} %copy.7.table, f32[2,5,32,256]{3,2,1,0:T(8,128)S(1)} %shard_map.71.low, f32[4,5,32,256]{3,2,1,0:T(8,128)S(1)} %collective-permute-done.5.middle, ...), custom_call_target="tpu_custom_call" | custom-call | tf_op jit(solution)/shard_map/pallas_call | solution.py:326
  (24 shorter events, 0.3 us)
Async XLA Ops:
  0.6 1.2 %copy-start = (f32[4,8,32,256]{3,2,1,0:T(8,128)S(1)}, f32[4,8,32,256]{3,2,1,0:T(8,128)}, u32[]{:S(2)}) copy-start(f32[4,8,32,256]{3,2,1,0:T(8,128)} %seed.1) | copy-start | bytes 3145732
  1.9 1.0 %copy-start.1 = (f32[2,8,32,256]{3,2,1,0:T(8,128)S(1)}, f32[2,8,32,256]{3,2,1,0:T(8,128)}, u32[]{:S(2)}) copy-start(f32[2,8,32,256]{3,2,1,0:T(8,128)} %potential.1) | copy-start | bytes 1572868
  2.9 0.9 %copy-start.4 = (s32[8,32,256]{2,1,0:T(8,128)S(1)}, s32[8,32,256]{2,1,0:T(8,128)}, u32[]{:S(2)}) copy-start(s32[8,32,256]{2,1,0:T(8,128)} %labels.1) | copy-start | bytes 786436
  4.8 37.9 %collective-permute-start = (f32[4,5,32,256]{3,2,1,0:T(8,128)}, f32[4,5,32,256]{3,2,1,0:T(8,128)S(1)}, u32[]{:S(2)}, u32[]{:S(2)}) collective-permute-start(f32[4,5,32,256]{3,2,1,0:T(8,128)} %get-tuple-element.10), channel_id=1, source_target_pairs={{0,504},{8,0},{16,8},{24,16},{32,24},{40,32},{48,40},{56,48},{64,5... | collective-permute-start | bytes 1966088 | tf_op jit(solution)/shard_map/ppermute | solution.py:252
  14.7 8.8 %collective-permute-start.3 = (f32[80,256]{1,0:T(8,128)S(1)}, f32[80,256]{1,0:T(8,128)S(1)}, u32[]{:S(2)}, u32[]{:S(2)}) collective-permute-start(f32[80,256]{1,0:T(8,128)S(1)} %get-tuple-element.12), channel_id=1, source_target_pairs={{0,7},{1,0},{2,1},{3,2},{4,3},{5,4},{6,5},{7,6},{8,15},{9,8},{10,9... | collective-permute-start | bytes 245768 | tf_op jit(solution)/shard_map/ppermute | solution.py:252
  17.6 10.0 %collective-permute-start.4 = (f32[80,256]{1,0:T(8,128)S(1)}, f32[80,256]{1,0:T(8,128)S(1)}, u32[]{:S(2)}, u32[]{:S(2)}) collective-permute-start(f32[80,256]{1,0:T(8,128)S(1)} %get-tuple-element.13), channel_id=1, source_target_pairs={{0,1},{1,2},{2,3},{3,4},{4,5},{5,6},{6,7},{7,0},{8,9},{9,10},{10,1... | collective-permute-start | bytes 245768 | tf_op jit(solution)/shard_map/ppermute | solution.py:252
  27.6 3.7 %copy-start.2 = (f32[80,256]{1,0:T(8,128)}, f32[80,256]{1,0:T(8,128)S(1)}, u32[]{:S(2)}) copy-start(f32[80,256]{1,0:T(8,128)S(1)} %collective-permute-done.4.before) | copy-start | bytes 245764
  31.3 41.2 %collective-permute-start.5 = (f32[4,5,32,256]{3,2,1,0:T(8,128)}, f32[4,5,32,256]{3,2,1,0:T(8,128)S(1)}, u32[]{:S(2)}, u32[]{:S(2)}) collective-permute-start(f32[4,5,32,256]{3,2,1,0:T(8,128)} %get-tuple-element.16), channel_id=1, source_target_pairs={{0,504},{8,0},{16,8},{24,16},{32,24},{40,32},{48,40},{56,48},{64,5... | collective-permute-start | bytes 1966088 | tf_op jit(solution)/shard_map/ppermute | solution.py:252
  42.8 6.5 %collective-permute-start.1 = (f32[40,256]{1,0:T(8,128)S(1)}, f32[40,256]{1,0:T(8,128)S(1)}, u32[]{:S(2)}, u32[]{:S(2)}) collective-permute-start(f32[40,256]{1,0:T(8,128)S(1)} %reshape.10), channel_id=1, source_target_pairs={{0,7},{1,0},{2,1},{3,2},{4,3},{5,4},{6,5},{7,6},{8,15},{9,8},{10,9... | collective-permute-start | bytes 122888 | tf_op jit(solution)/shard_map/ppermute | solution.py:252
  44.8 5.6 %collective-permute-start.2 = (f32[40,256]{1,0:T(8,128)S(1)}, f32[40,256]{1,0:T(8,128)S(1)}, u32[]{:S(2)}, u32[]{:S(2)}) collective-permute-start(f32[40,256]{1,0:T(8,128)S(1)} %reshape.11), channel_id=1, source_target_pairs={{0,1},{1,2},{2,3},{3,4},{4,5},{5,6},{6,7},{7,0},{8,9},{9,10},{10,1... | collective-permute-start | bytes 122888 | tf_op jit(solution)/shard_map/ppermute | solution.py:252
  49.3 0.6 copy-start.6
  50.4 3.9 %copy-start.9 = (f32[40,256]{1,0:T(8,128)}, f32[40,256]{1,0:T(8,128)S(1)}, u32[]{:S(2)}) copy-start(f32[40,256]{1,0:T(8,128)S(1)} %collective-permute-done.2.upper_before) | copy-start | bytes 122884
  50.4 0.9 %copy-start.3 = (f32[80,256]{1,0:T(8,128)S(1)}, f32[80,256]{1,0:T(8,128)}, u32[]{:S(2)}) copy-start(f32[80,256]{1,0:T(8,128)} %copy-done.2) | copy-start | bytes 245764
  51.3 0.8 %copy-start.7 = (f32[40,256]{1,0:T(8,128)S(1)}, f32[40,256]{1,0:T(8,128)}, u32[]{:S(2)}) copy-start(f32[40,256]{1,0:T(8,128)} %copy-done.6) | copy-start | bytes 122884
  52.1 17.3 %copy-start.11 = (f32[16,2]{0,1:T(2,128)S(1)}, f32[16,2]{0,1:T(2,128)}, u32[]{:S(2)}) copy-start(f32[16,2]{0,1:T(2,128)} %param.9) | copy-start | bytes 388
  54.3 19.4 %copy-start.5 = (s32[8,32,256]{2,1,0:T(8,128)S(1)}, s32[8,32,256]{2,1,0:T(8,128)}, u32[]{:S(2)}) copy-start(s32[8,32,256]{2,1,0:T(8,128)} %inflow.1) | copy-start | bytes 786436
  54.3 19.4 %collective-permute-start.6 = (f32[2,5,32,256]{3,2,1,0:T(8,128)}, f32[2,5,32,256]{3,2,1,0:T(8,128)S(1)}, u32[]{:S(2)}, u32[]{:S(2)}) collective-permute-start(f32[2,5,32,256]{3,2,1,0:T(8,128)} %get-tuple-element.17), channel_id=1, source_target_pairs={{0,504},{8,0},{16,8},{24,16},{32,24},{40,32},{48,40},{56,48},{64,5... | collective-permute-start | bytes 983048 | tf_op jit(solution)/shard_map/ppermute | solution.py:252
  69.5 0.8 %copy-start.8 = (f32[40,256]{1,0:T(8,128)S(1)}, f32[40,256]{1,0:T(8,128)}, u32[]{:S(2)}) copy-start(f32[40,256]{1,0:T(8,128)} %copy-done.6) | copy-start | bytes 122884
  70.3 0.8 %copy-start.10 = (f32[40,256]{1,0:T(8,128)S(1)}, f32[40,256]{1,0:T(8,128)}, u32[]{:S(2)}) copy-start(f32[40,256]{1,0:T(8,128)} %copy-done.9) | copy-start | bytes 122884

commit v2 on v1

v2 whole, which is shorter than its diff:
```python
import functools

import jax
import jax.numpy as jnp
from jax import lax
from jax.experimental import pallas as pl
from jax.experimental.pallas import tpu as pltpu
from jax.sharding import PartitionSpec as P

offset_table = ((0.0, 0.0), (0.6, -0.3), (-0.4, 0.5), (-0.2, -0.6))
latent_heat = (0.0, 0.8, 0.8, 0.8)
relax_rate = 0.1
diffusion = 0.05

shift = 3
early = 2
fields = 5
tile = 8
edge_size = -(-2 * fields * (shift + 2) // tile) * tile

VMEM = pl.BlockSpec(memory_space=pltpu.VMEM)
SMEM = pl.BlockSpec(memory_space=pltpu.SMEM)
ANY = pl.BlockSpec(memory_space=pl.ANY)


def step_tile(below, above, centre, before, after, temp):
    row = lax.broadcasted_iota(jnp.int32, centre[0].shape, 0)
    last = centre[0].shape[0] - 1
    width = centre[0].shape[1]
    laps = []
    for f in range(fields):
        c = centre[f]
        x_minus = pltpu.roll(jnp.where(row == last, before[f], c), 1, 0)
        x_plus = pltpu.roll(jnp.where(row == 0, after[f], c), last, 0)
        y_minus = pltpu.roll(c, 1, 1)
        y_plus = pltpu.roll(c, width - 1, 1)
        laps.append(
            (above[f] + below[f]) + (x_plus + x_minus) + (y_plus + y_minus) - 6.0 * c
        )
    p = list(centre[:3])
    p.append(1.0 - (p[0] + p[1] + p[2]))
    mu = centre[3:]
    common = 1.0 - (mu[0] * mu[0] + mu[1] * mu[1])
    react = []
    for a in range(4):
        e0, e1 = offset_table[a]
        w = common
        if a:
            w = w - (2.0 * e0) * mu[0] - (2.0 * e1) * mu[1]
            w = w + (2.0 * latent_heat[a] * temp - (e0 * e0 + e1 * e1))
        react.append(p[a] * (w + p[a] * (2.0 * p[a] - 3.0)))
    mean = 0.25 * ((react[0] + react[1]) + (react[2] + react[3]))
    new = [p[a] + relax_rate * (laps[a] + (mean - react[a])) for a in range(3)]
    new.append(1.0 - (new[0] + new[1] + new[2]))
    squares = [n * n for n in new]
    growth = [squares[a] - p[a] * p[a] for a in range(4)]
    sus = (squares[0] + squares[1]) + (squares[2] + squares[3])
    grown = (growth[0] + growth[1]) + (growth[2] + growth[3])
    mobile = diffusion * 0.1 + diffusion * squares[0]
    inverse = 1.0 / sus
    out = new[:3]
    for k in range(2):
        source = mu[k] * grown
        for a in range(1, 4):
            source = source + offset_table[a][k] * growth[a]
        out.append(mu[k] + (mobile * laps[3 + k] - source) * inverse)
    return out


def step_plane(src, at, dst, to, temp, tiles, all_tiles):
    for t in range(tiles):
        def rows(plane, u):
            u = (u + all_tiles) % all_tiles
            return [src[plane, f, u * tile : (u + 1) * tile, :] for f in range(fields)]

        new = step_tile(
            rows(at - 1, t), rows(at + 1, t), rows(at, t), rows(at, t - 1), rows(at, t + 1), temp
        )
        for f in range(fields):
            dst[to, f, t * tile : (t + 1) * tile, :] = new[f]


def temp_of(z, planes):
    plane = (lax.axis_index("grow") * planes + z).astype(jnp.float32)
    return 2.0 * (plane + 0.5) / float(lax.axis_size("grow") * planes) - 1.0


def is_even():
    return lax.rem(lax.axis_index("lat"), 2) == 0


def is_top():
    return lax.axis_index("grow") == lax.axis_size("grow") - 1


def load_planes(labels, seed, potential, lab, blend, mu, sems, first, count, at):
    zs, to = (pl.ds(first, count), pl.ds(at, count))
    copies = [
        pltpu.make_async_copy(seed.at[:, zs], blend.at[:, to], sems.at[0]),
        pltpu.make_async_copy(labels.at[zs], lab.at[to], sems.at[1]),
        pltpu.make_async_copy(potential.at[:, zs], mu.at[:, to], sems.at[2]),
    ]
    for copy in copies:
        copy.start()
    return copies


def initial_plane(kind, blend, mu, z):
    total = 1.0 + ((blend[0, z] + blend[1, z]) + (blend[2, z] + blend[3, z]))
    scale = 1.0 / total
    vals = [(jnp.where(kind[z] == a, 1.0, 0.0) + blend[a, z]) * scale for a in range(3)]
    return vals + [mu[0, z], mu[1, z]]


def first_kernel(labels, seed, potential, near, token, lab, blend, mu, sems):
    token[...] = jnp.zeros_like(token)
    for copy in load_planes(labels, seed, potential, lab, blend, mu, sems, 0, early, 0):
        copy.wait()
    for z in range(early):
        for f, value in enumerate(initial_plane(lab, blend, mu, z)):
            near[z, f] = value


def start_kernel(labels, seed, potential, token, state, far, inner, outer):
    planes, height = labels.shape[0], labels.shape[1]
    for z in range(planes):
        vals = initial_plane(labels, seed, potential, z)
        for f in range(fields):
            state[z, f] = vals[f]
            if early <= z < shift + 2:
                at = ((z - early) * fields + f) * height
                far[at : at + height, :] = vals[f]

    def edges(after, before):
        for z in range(planes):
            for f in range(fields):
                at = 2 * (z * fields + f)
                before[at : at + 2, :] = state[z, f, 0:2, :]
                after[at : at + 2, :] = state[z, f, height - 2 : height, :]

    @pl.when(is_even())
    def _():
        edges(inner, outer)

    @pl.when(jnp.logical_not(is_even()))
    def _():
        edges(outer, inner)


def pack_kernel(far, inner, outer, near, done, sems):
    at = far.shape[0] - 2 * edge_size
    slot = jnp.where(is_even(), 0, inner.shape[0])
    copies = [
        pltpu.make_async_copy(inner.at[0:edge_size], done.at[at : at + edge_size], sems.at[0]),
        pltpu.make_async_copy(
            outer.at[pl.ds(pl.multiple_of(slot, tile), edge_size)], done.at[at + edge_size :], sems.at[1]
        ),
    ]
    for copy in copies:
        copy.start()
    for copy in copies:
        copy.wait()


def gather_planes(dst, places, height):
    for i, (main, z, _, _) in enumerate(places):
        if len(main.shape) == 4:
            dst[i, :, 0:height, :] = main[z]
        else:
            for f in range(fields):
                dst[i, f, 0:height, :] = main[(z + f) * height : (z + f + 1) * height, :]

    def halo(inner_row, outer_row, slot):
        for i, (_, _, rows, (at_inner, at_outer)) in enumerate(places):
            at_outer = at_outer[slot]
            for f in range(fields):
                for row, at, ref in ((inner_row, at_inner, rows[0]), (outer_row, at_outer, rows[1])):
                    dst[i, f, height + row : height + row + 2, :] = ref[at + 2 * f : at + 2 * f + 2, :]

    @pl.when(is_even())
    def _():
        halo(0, 6, 0)

    @pl.when(jnp.logical_not(is_even()))
    def _():
        halo(6, 0, 1)


def own_places(state, inner, outer, zs):
    width = 2 * fields
    slots = (0, inner.shape[0])
    return [(state, z, (inner, outer), (width * z, [at + width * z for at in slots])) for z in zs]


def upper_places(near, late, zs):
    height = near.shape[2]
    width = 2 * fields
    inner = (shift + 2 - early) * fields * height
    outer = inner + edge_size
    return [
        (near if z < early else late, z if z < early else (z - early) * fields, (late, late),
         (inner + width * z, [outer + width * z] * 2))
        for z in zs
    ]


def steps(padded, half, done, planes, first, known, count, all_tiles):
    def one(i, _):
        step_plane(padded, i + 1, half, i + known, temp_of(i + first - 1 + known, planes), all_tiles, all_tiles)
        return 0

    def two(i, _):
        step_plane(half, i + 1, done, i, temp_of(i + first, planes), all_tiles - 1, all_tiles)
        return 0

    return (
        lambda: lax.fori_loop(0, count + 2 - known, one, 0),
        lambda: lax.fori_loop(0, count, two, 0),
    )


def own_kernel(state, inner, outer, done, carry, padded, half):
    planes, height = state.shape[0], state.shape[2]
    gather_planes(padded, own_places(state, inner, outer, range(shift - 2, planes)), height)
    count = planes - 2 - shift
    one, two = steps(padded, half, done, planes, shift, 0, count, height // tile + 1)
    one()
    two()
    carry[...] = half[count : count + 2]


def edge_kernel(state, inner, outer, near, late, carry, done, carry_out, padded, half):
    planes, height = state.shape[0], state.shape[2]
    gather_planes(
        padded,
        own_places(state, inner, outer, range(planes - 2, planes)) + upper_places(near, late, range(2)),
        height,
    )
    one, two = steps(padded, half, done, planes, planes - 2, 2, 2, height // tile + 1)
    half[0:2] = carry[...]

    @pl.when(is_top())
    def _():
        padded[2] = padded[1]

    one()

    @pl.when(is_top())
    def _():
        half[3] = half[2]

    two()
    carry_out[...] = half[2:4]


def write_planes(parts, phase, chem, extra, sems):
    copies = []
    for part, first in parts:
        count = part.shape[0]
        for f in range(fields):
            to = pl.ds(first, count)
            dst = phase.at[f, to] if f < 3 else chem.at[f - 3, to]
            copies.append(pltpu.make_async_copy(part.at[:, f], dst, sems.at[len(copies)]))
            copies[-1].start()
    for part, first in parts:
        for z in range(part.shape[0]):
            extra[first - parts[0][1] + z] = 1.0 - (part[z, 0] + part[z, 1] + part[z, 2])
    count = sum(part.shape[0] for part, _ in parts)
    copies.append(
        pltpu.make_async_copy(extra.at[0:count], phase.at[3, pl.ds(parts[0][1], count)], sems.at[len(copies)])
    )
    copies[-1].start()
    for copy in copies:
        copy.wait()


def write_liquid(inflow, table, phase, chem, liquid, first, count, sems):
    shape = (count,) + liquid.shape[2:]
    liquid[0, 0:count] = jnp.ones(shape, jnp.float32)
    liquid[1, 0:count] = jnp.zeros(shape, jnp.float32)

    def lookup(z, _):
        kind = inflow[first + z]
        for k in range(2):
            value = jnp.zeros(kind.shape, jnp.float32)
            for j in range(table.shape[0]):
                value = jnp.where(kind == j, table[j, k], value)
            liquid[2 + k, z] = value
        return 0

    lax.fori_loop(0, count, lookup, 0)
    to = pl.ds(first, count)
    pairs = [(0, phase.at[0, to])] + [(1, phase.at[a, to]) for a in range(1, 4)]
    pairs += [(2 + k, chem.at[k, to]) for k in range(2)]
    copies = [pltpu.make_async_copy(liquid.at[j, 0:count], dst, sems.at[i]) for i, (j, dst) in enumerate(pairs)]
    for copy in copies:
        copy.start()
    for copy in copies:
        copy.wait()


def upper_kernel(table, near, late, carry, middle, inflow, phase, chem, padded, half, low, liquid, sems):
    planes, height = phase.shape[1], near.shape[2]

    @pl.when(jnp.logical_not(is_top()))
    def _():
        gather_planes(padded, upper_places(near, late, range(shift + 2)), height)
        half[0:2] = carry[...]
        one, two = steps(padded, half, low, planes, planes, 2, shift, height // tile + 1)
        one()
        two()
        write_planes([(low, 0), (middle, shift)], phase, chem, liquid.at[0], sems)

    @pl.when(is_top())
    def _():
        write_liquid(inflow, table, phase, chem, liquid, 0, planes - 2, sems)


def last_kernel(table, high, inflow, phase_in, chem_in, phase, chem, liquid, sems):
    planes = phase.shape[1]

    @pl.when(jnp.logical_not(is_top()))
    def _():
        write_planes([(high, planes - 2)], phase, chem, liquid.at[0], sems)

    @pl.when(is_top())
    def _():
        write_liquid(inflow, table, phase, chem, liquid, planes - 2, 2, sems)


def f32(*shape):
    return jax.ShapeDtypeStruct(shape, jnp.float32)


def down(block):
    return lax.ppermute(block, "grow", [(i, i - 1) for i in range(1, lax.axis_size("grow"))])


def call(kernel, out_shape, in_specs, scratch=(), out_specs=None, aliases={}, grant=10):
    return pl.pallas_call(
        kernel,
        out_shape=out_shape,
        in_specs=in_specs,
        out_specs=out_specs if out_specs is not None else jax.tree.map(lambda _: VMEM, out_shape),
        scratch_shapes=list(scratch),
        input_output_aliases=aliases,
        compiler_params=pltpu.CompilerParams(vmem_limit_bytes=grant * 1024 * 1024),
    )


def body(labels, seed_blend, potential, inflow_index, liquid_table):
    planes, height, width = labels.shape
    count = lax.axis_size("lat")
    padded_rows = height + tile

    def room(*shape):
        return pltpu.VMEM(shape, jnp.float32)

    near, token = call(
        first_kernel,
        (f32(early, fields, height, width), f32(tile, 128)),
        [ANY] * 3,
        [
            pltpu.VMEM((early, height, width), jnp.int32),
            room(4, early, height, width),
            room(2, early, height, width),
            pltpu.SemaphoreType.DMA((3,)),
        ],
        grant=56,
    )(labels, seed_blend, potential)
    near = down(near)

    edge_rows = 2 * planes * fields
    state, far, inner, outer = call(
        start_kernel,
        (
            f32(planes, fields, height, width),
            f32((shift + 2 - early) * fields * height + 2 * edge_size, width),
            f32(edge_rows, width),
            f32(edge_rows, width),
        ),
        [VMEM] * 3 + [ANY],
    )(labels, seed_blend, potential, token)

    inner = lax.ppermute(inner, "lat", [(i, i ^ 1) for i in range(count)])
    pairs = [[i, (i + 1) % count] for i in range(1, count, 2)]
    outer = lax.all_gather(outer, "lat", axis_index_groups=pairs, tiled=True)
    late = call(
        pack_kernel,
        jax.ShapeDtypeStruct(far.shape, far.dtype),
        [ANY] * 4,
        [pltpu.SemaphoreType.DMA((2,))],
        ANY,
        aliases={0: 0},
    )(far, inner, outer, near)
    late = down(late)

    middle, carry = call(
        own_kernel,
        (f32(planes - 2 - shift, fields, height, width), f32(2, fields, padded_rows, width)),
        [VMEM] * 3,
        [room(planes - shift + 2, fields, padded_rows, width), room(planes - shift, fields, padded_rows, width)],
    )(state, inner, outer)
    middle = down(middle)

    high, carry = call(
        edge_kernel,
        (f32(2, fields, height, width), f32(2, fields, padded_rows, width)),
        [VMEM] * 6,
        [room(4, fields, padded_rows, width), room(4, fields, padded_rows, width)],
    )(state, inner, outer, near, late, carry)
    high = down(high)

    outs = (f32(4, planes, height, width), f32(2, planes, height, width))
    phase, chem = call(
        upper_kernel,
        outs,
        [SMEM] + [VMEM] * 5,
        [
            room(shift + 2, fields, padded_rows, width),
            room(shift + 2, fields, padded_rows, width),
            room(shift, fields, height, width),
            room(4, planes - 2, height, width),
            pltpu.SemaphoreType.DMA((2 * fields + 1,)),
        ],
        (ANY, ANY),
    )(liquid_table, near, late, carry, middle, inflow_index)
    return call(
        last_kernel,
        outs,
        [SMEM] + [VMEM] * 2 + [ANY] * 2,
        [room(4, 2, height, width), pltpu.SemaphoreType.DMA((fields + 1,))],
        (ANY, ANY),
        aliases={3: 0, 4: 1},
    )(liquid_table, high, inflow_index, phase, chem)


def solution(mesh):
    in_specs = (
        P("grow", "lat", None),
        P(None, "grow", "lat", None),
        P(None, "grow", "lat", None),
        P(None, "lat", None),
        P(),
    )
    out_specs = (P(None, "grow", "lat", None), P(None, "grow", "lat", None))
    return jax.shard_map(body, mesh=mesh, in_specs=in_specs, out_specs=out_specs, check_vma=False)
```

time: 76.3 us -> 60 us (0.79)
  the two profiles are of different devices: /device:TPU:1 before, /device:TPU:6 now
where the time goes in v2:
time: 60 us; the launch traced here: 59.7 us
  starting transfers between devices  23.6 us (39%)
  waiting for transfers between devices  13.1 us (22%)
  blocking collectives  11.5 us (19%)
  Pallas kernels  9.87 us (16%)
  local copies, waits for them, and re-layouts  0.79 us (1%)
  between operations  0.78 us (1%)
    ppermute x4, starting transfers between devices, down(): lax.ppermute(block, 'grow', [(i, i - 1) for i in range(1, lax.axis_size('...  21.7 us
    ppermute x4, waiting for transfers between devices, down(): lax.ppermute(block, 'grow', [(i, i - 1) for i in range(1, lax.axis_size('...  13.1 us
    all_gather x1, blocking collectives, body(): outer = lax.all_gather(outer, 'lat', axis_index_groups=pairs, tiled=True)  11.5 us
    pallas_call x1, Pallas kernels, body(): call(upper_kernel, outs, [SMEM] + [VMEM] * 5, [room(shift + 2, fields, pa...  3.18 us
    pallas_call x1, Pallas kernels, body(): call(first_kernel, (f32(early, fields, height, width), f32(tile, 128)), [...  1.94 us
    ppermute x1, starting transfers between devices, body(): inner = lax.ppermute(inner, 'lat', [(i, i ^ 1) for i in range(count)])  1.92 us
    pallas_call x1, Pallas kernels, body(): call(own_kernel, (f32(planes - 2 - shift, fields, height, width), f32(2,...  1.92 us
    pallas_call x1, Pallas kernels, body(): call(last_kernel, outs, [SMEM] + [VMEM] * 2 + [ANY] * 2, [room(4, 2, heig...  1.46 us
  transfers between devices with their start and end apart: 5, of which 3 were waited for; matrix products, arithmetic and copies ran while one was open for 0% of the time, Pallas kernels for 11%

profile of v2, /device:TPU:6, one launch (start us, length us, event | category | flops | bytes accessed | tf_op | source)
XLA Modules:
  0.0 59.7 jit_solution(2440821372547376448)
XLA Ops:
  0.6 0.0 copy-start.2
  0.6 0.0 copy-start
  0.7 1.9 %shard_map.68 = (f32[2,5,32,256]{3,2,1,0:T(8,128)}, f32[8,128]{1,0:T(8,128)}) custom-call(s32[8,32,256]{2,1,0:T(8,128)} %labels.3, f32[4,8,32,256]{3,2,1,0:T(8,128)} %seed.3, f32[2,8,32,256]{3,2,1,0:T(8,128)} %potential.3), custom_call_target="tpu_custom_call" | custom-call | tf_op jit(solution)/shard_map/pallas_call | solution.py:359
  2.6 7.5 %collective-permute-start.1 = (f32[2,5,32,256]{3,2,1,0:T(8,128)}, f32[2,5,32,256]{3,2,1,0:T(8,128)S(1)}, u32[]{:S(2)}, u32[]{:S(2)}) collective-permute-start(f32[2,5,32,256]{3,2,1,0:T(8,128)} %get-tuple-element.18), channel_id=1, source_target_pairs={{8,0},{16,8},{24,16},{32,24},{40,32},{48,40},{56,48},{64,56},{72,6... | collective-permute-start | bytes 983048 | tf_op jit(solution)/shard_map/ppermute | solution.py:336
  10.1 0.0 copy-start.4
  10.1 0.7 %copy-done.4 = f32[8,128]{1,0:T(8,128)S(1)} copy-done((f32[8,128]{1,0:T(8,128)S(1)}, f32[8,128]{1,0:T(8,128)}, u32[]{:S(2)}) %copy-start.4) | copy-done | bytes 4120
  10.8 0.2 shard_map.69
  11.0 1.9 %collective-permute-start = (f32[80,256]{1,0:T(8,128)S(1)}, f32[80,256]{1,0:T(8,128)S(1)}, u32[]{:S(2)}, u32[]{:S(2)}) collective-permute-start(f32[80,256]{1,0:T(8,128)S(1)} %get-tuple-element.16), channel_id=1, source_target_pairs={{0,1},{1,0},{2,3},{3,2},{4,5},{5,4},{6,7},{7,6},{8,9},{9,8},{10,11... | collective-permute-start | bytes 245768 | tf_op jit(solution)/shard_map/ppermute | solution.py:385
  12.9 11.5 %all_gather.3.outer = f32[160,256]{1,0:T(8,128)S(1)} all-gather(f32[80,256]{1,0:T(8,128)S(1)} %get-tuple-element.17), channel_id=1, replica_groups={{1,2},{3,4},{5,6},{7,0},{9,10},{11,12},{13,14},{15,8},{17,18},{19,20},{..., dimensions={0}, use_global_device_ids=true | all-gather | bytes 245760 | tf_op jit(solution)/shard_map/all_gather | solution.py:387
  24.4 0.0 collective-permute-done.inner
  24.4 0.0 collective-permute-done.1.near
  24.4 0.2 shard_map.70
  24.6 2.9 %collective-permute-start.2 = (f32[592,256]{1,0:T(8,128)S(1)}, f32[592,256]{1,0:T(8,128)S(1)}, u32[]{:S(2)}, u32[]{:S(2)}) collective-permute-start(f32[592,256]{1,0:T(8,128)S(1)} %shard_map.70), channel_id=1, source_target_pairs={{8,0},{16,8},{24,16},{32,24},{40,32},{48,40},{56,48},{64,56},{72,6... | collective-permute-start | bytes 1818632 | tf_op jit(solution)/shard_map/ppermute | solution.py:336
  27.5 1.9 %shard_map.71 = (f32[3,5,32,256]{3,2,1,0:T(8,128)S(1)}, f32[2,5,40,256]{3,2,1,0:T(8,128)S(1)}) custom-call(f32[8,5,32,256]{3,2,1,0:T(8,128)S(1)} %get-tuple-element.15.state, f32[80,256]{1,0:T(8,128)S(1)} %collective-permute-done.inner, f32[160,256]{1,0:T(8,128)S(1)} %all_gather.3.outer), custom_call_target="tpu_custom_call" | custom-call | tf_op jit(solution)/shard_map/pallas_call | solution.py:398
  29.4 4.0 %collective-permute-start.4 = (f32[3,5,32,256]{3,2,1,0:T(8,128)S(1)}, f32[3,5,32,256]{3,2,1,0:T(8,128)S(1)}, u32[]{:S(2)}, u32[]{:S(2)}) collective-permute-start(f32[3,5,32,256]{3,2,1,0:T(8,128)S(1)} %get-tuple-element.23), channel_id=1, source_target_pairs={{8,0},{16,8},{24,16},{32,24},{40,32},{48,40},{56,48},{64,56},{72,6... | collective-permute-start | bytes 1474568 | tf_op jit(solution)/shard_map/ppermute | solution.py:336
  33.4 8.1 %collective-permute-done.2.late = f32[592,256]{1,0:T(8,128)S(1)} collective-permute-done((f32[592,256]{1,0:T(8,128)S(1)}, f32[592,256]{1,0:T(8,128)S(1)}, u32[]{:S(2)}, u32[]{:S(2)}) %collective-permute-start.2) | collective-permute-done | bytes 606240 | tf_op jit(solution)/shard_map/ppermute | solution.py:336
  41.6 1.0 %shard_map.72 = (f32[2,5,32,256]{3,2,1,0:T(8,128)S(1)}, f32[2,5,40,256]{3,2,1,0:T(8,128)S(1)}) custom-call(f32[8,5,32,256]{3,2,1,0:T(8,128)S(1)} %get-tuple-element.15.state, f32[80,256]{1,0:T(8,128)S(1)} %collective-permute-done.inner, f32[160,256]{1,0:T(8,128)S(1)} %all_gather.3.outer, f32[2,5,32,256]{3,2,1,0:T(8,128)S(1)} %collective-permute-done.1.near, ...), custom_call_target="tpu_custom_call" | custom-call | tf_op jit(solution)/shard_map/pallas_call | solution.py:406
  42.6 7.3 %collective-permute-start.3 = (f32[2,5,32,256]{3,2,1,0:T(8,128)S(1)}, f32[2,5,32,256]{3,2,1,0:T(8,128)S(1)}, u32[]{:S(2)}, u32[]{:S(2)}) collective-permute-start(f32[2,5,32,256]{3,2,1,0:T(8,128)S(1)} %get-tuple-element.21), channel_id=1, source_target_pairs={{8,0},{16,8},{24,16},{32,24},{40,32},{48,40},{56,48},{64,56},{72,6... | collective-permute-start | bytes 983048 | tf_op jit(solution)/shard_map/ppermute | solution.py:336
  49.9 0.0 copy-done.5
  49.9 0.1 copy.11.table
  50.0 2.0 %collective-permute-done.4.middle = f32[3,5,32,256]{3,2,1,0:T(8,128)S(1)} collective-permute-done((f32[3,5,32,256]{3,2,1,0:T(8,128)S(1)}, f32[3,5,32,256]{3,2,1,0:T(8,128)S(1)}, u32[]{:S(2)}, u32[]{:S(2)}) %collective-permute-start.4) | collective-permute-done | bytes 491552 | tf_op jit(solution)/shard_map/ppermute | solution.py:336
  52.1 3.2 %shard_map.73 = (f32[4,8,32,256]{3,2,1,0:T(8,128)}, f32[2,8,32,256]{3,2,1,0:T(8,128)}) custom-call(f32[16,2]{1,0:T(8,128)S(1)} %copy.11.table, f32[2,5,32,256]{3,2,1,0:T(8,128)S(1)} %collective-permute-done.1.near, f32[592,256]{1,0:T(8,128)S(1)} %collective-permute-done.2.late, f32[2,5,40,256]{3,2,1,0:T(8,128)S(1)} %get-tuple-element.22.carry, ...), custom_call_target="tpu_custom_call" | custom-call | tf_op jit(solution)/shard_map/pallas_call | solution.py:415
  55.2 3.0 %collective-permute-done.3.high = f32[2,5,32,256]{3,2,1,0:T(8,128)S(1)} collective-permute-done((f32[2,5,32,256]{3,2,1,0:T(8,128)S(1)}, f32[2,5,32,256]{3,2,1,0:T(8,128)S(1)}, u32[]{:S(2)}, u32[]{:S(2)}) %collective-permute-start.3) | collective-permute-done | bytes 327712 | tf_op jit(solution)/shard_map/ppermute | solution.py:336
  58.2 1.5 %shard_map.74 = (f32[4,8,32,256]{3,2,1,0:T(8,128)}, f32[2,8,32,256]{3,2,1,0:T(8,128)}) custom-call(f32[16,2]{1,0:T(8,128)S(1)} %copy.11.table, f32[2,5,32,256]{3,2,1,0:T(8,128)S(1)} %collective-permute-done.3.high, s32[8,32,256]{2,1,0:T(8,128)S(1)} %copy-done.3, ...), custom_call_target="tpu_custom_call", output_to_operand_aliasing={{0}: (3, {}), {1}: (4, {})} | custom-call | tf_op jit(solution)/shard_map/pallas_call | solution.py:428
  (7 shorter events, 0.0 us)
Async XLA Ops:
  0.6 9.4 %copy-start.2 = (s32[8,32,256]{2,1,0:T(8,128)S(1)}, s32[8,32,256]{2,1,0:T(8,128)}, u32[]{:S(2)}) copy-start(s32[8,32,256]{2,1,0:T(8,128)} %labels.3) | copy-start | bytes 786436
  0.6 9.4 %copy-start = (f32[4,8,32,256]{3,2,1,0:T(8,128)S(1)}, f32[4,8,32,256]{3,2,1,0:T(8,128)}, u32[]{:S(2)}) copy-start(f32[4,8,32,256]{3,2,1,0:T(8,128)} %seed.3) | copy-start | bytes 3145732
  0.6 9.4 %copy-start.1 = (f32[2,8,32,256]{3,2,1,0:T(8,128)S(1)}, f32[2,8,32,256]{3,2,1,0:T(8,128)}, u32[]{:S(2)}) copy-start(f32[2,8,32,256]{3,2,1,0:T(8,128)} %potential.3) | copy-start | bytes 1572868
  2.6 21.8 %collective-permute-start.1 = (f32[2,5,32,256]{3,2,1,0:T(8,128)}, f32[2,5,32,256]{3,2,1,0:T(8,128)S(1)}, u32[]{:S(2)}, u32[]{:S(2)}) collective-permute-start(f32[2,5,32,256]{3,2,1,0:T(8,128)} %get-tuple-element.18), channel_id=1, source_target_pairs={{8,0},{16,8},{24,16},{32,24},{40,32},{48,40},{56,48},{64,56},{72,6... | collective-permute-start | bytes 983048 | tf_op jit(solution)/shard_map/ppermute | solution.py:336
  10.1 0.7 %copy-start.4 = (f32[8,128]{1,0:T(8,128)S(1)}, f32[8,128]{1,0:T(8,128)}, u32[]{:S(2)}) copy-start(f32[8,128]{1,0:T(8,128)} %get-tuple-element.14.token) | copy-start | bytes 12292
  11.0 13.4 %collective-permute-start = (f32[80,256]{1,0:T(8,128)S(1)}, f32[80,256]{1,0:T(8,128)S(1)}, u32[]{:S(2)}, u32[]{:S(2)}) collective-permute-start(f32[80,256]{1,0:T(8,128)S(1)} %get-tuple-element.16), channel_id=1, source_target_pairs={{0,1},{1,0},{2,3},{3,2},{4,5},{5,4},{6,7},{7,6},{8,9},{9,8},{10,11... | collective-permute-start | bytes 245768 | tf_op jit(solution)/shard_map/ppermute | solution.py:385
  24.6 16.9 %collective-permute-start.2 = (f32[592,256]{1,0:T(8,128)S(1)}, f32[592,256]{1,0:T(8,128)S(1)}, u32[]{:S(2)}, u32[]{:S(2)}) collective-permute-start(f32[592,256]{1,0:T(8,128)S(1)} %shard_map.70), channel_id=1, source_target_pairs={{8,0},{16,8},{24,16},{32,24},{40,32},{48,40},{56,48},{64,56},{72,6... | collective-permute-start | bytes 1818632 | tf_op jit(solution)/shard_map/ppermute | solution.py:336
  29.4 22.6 %collective-permute-start.4 = (f32[3,5,32,256]{3,2,1,0:T(8,128)S(1)}, f32[3,5,32,256]{3,2,1,0:T(8,128)S(1)}, u32[]{:S(2)}, u32[]{:S(2)}) collective-permute-start(f32[3,5,32,256]{3,2,1,0:T(8,128)S(1)} %get-tuple-element.23), channel_id=1, source_target_pairs={{8,0},{16,8},{24,16},{32,24},{40,32},{48,40},{56,48},{64,56},{72,6... | collective-permute-start | bytes 1474568 | tf_op jit(solution)/shard_map/ppermute | solution.py:336
  41.6 8.3 %copy-start.5 = (f32[16,2]{0,1:T(2,128)S(1)}, f32[16,2]{0,1:T(2,128)}, u32[]{:S(2)}) copy-start(f32[16,2]{0,1:T(2,128)} %param.9) | copy-start | bytes 388
  41.6 10.5 %copy-start.3 = (s32[8,32,256]{2,1,0:T(8,128)S(1)}, s32[8,32,256]{2,1,0:T(8,128)}, u32[]{:S(2)}) copy-start(s32[8,32,256]{2,1,0:T(8,128)} %inflow.3) | copy-start | bytes 786436
  42.6 15.7 %collective-permute-start.3 = (f32[2,5,32,256]{3,2,1,0:T(8,128)S(1)}, f32[2,5,32,256]{3,2,1,0:T(8,128)S(1)}, u32[]{:S(2)}, u32[]{:S(2)}) collective-permute-start(f32[2,5,32,256]{3,2,1,0:T(8,128)S(1)} %get-tuple-element.21), channel_id=1, source_target_pairs={{8,0},{16,8},{24,16},{32,24},{40,32},{48,40},{56,48},{64,56},{72,6... | collective-permute-start | bytes 983048 | tf_op jit(solution)/shard_map/ppermute | solution.py:336

commit v3 on v2

--- a/solution.py
+++ b/solution.py
@@ -12,8 +12,8 @@
 relax_rate = 0.1
 diffusion = 0.05
 
-shift = 3
-early = 2
+shift = 2
+early = 1
 fields = 5
 tile = 8
 edge_size = -(-2 * fields * (shift + 2) // tile) * tile
@@ -112,8 +112,7 @@
     return vals + [mu[0, z], mu[1, z]]
 
 
-def first_kernel(labels, seed, potential, near, token, lab, blend, mu, sems):
-    token[...] = jnp.zeros_like(token)
+def first_kernel(labels, seed, potential, near, lab, blend, mu, sems):
     for copy in load_planes(labels, seed, potential, lab, blend, mu, sems, 0, early, 0):
         copy.wait()
     for z in range(early):
@@ -121,7 +120,7 @@
             near[z, f] = value
 
 
-def start_kernel(labels, seed, potential, token, state, far, inner, outer):
+def start_kernel(labels, seed, potential, state, far, inner, outer):
     planes, height = labels.shape[0], labels.shape[1]
     for z in range(planes):
         vals = initial_plane(labels, seed, potential, z)
@@ -356,9 +355,9 @@
     def room(*shape):
         return pltpu.VMEM(shape, jnp.float32)
 
-    near, token = call(
+    near = call(
         first_kernel,
-        (f32(early, fields, height, width), f32(tile, 128)),
+        f32(early, fields, height, width),
         [ANY] * 3,
         [
             pltpu.VMEM((early, height, width), jnp.int32),
@@ -379,8 +378,8 @@
             f32(edge_rows, width),
             f32(edge_rows, width),
         ),
-        [VMEM] * 3 + [ANY],
-    )(labels, seed_blend, potential, token)
+        [VMEM] * 3,
+    )(labels, seed_blend, potential)
 
     inner = lax.ppermute(inner, "lat", [(i, i ^ 1) for i in range(count)])
     pairs = [[i, (i + 1) % count] for i in range(1, count, 2)]

time: 60 us -> 58.8 us (0.980)
  starting transfers between devices: 23.6 us -> 22.1 us
  waiting for transfers between devices: 13.1 us -> 14.4 us
  local copies, waits for them, and re-layouts: 0.79 us -> 0.1 us
    ppermute x4, starting transfers between devices: 21.7 us -> 20.2 us  [down(): lax.ppermute(block, 'grow', [(i, i - 1) for i in range(1, lax.axis_size('...]
    ppermute x4, waiting for transfers between devices: 13.1 us -> 14.4 us  [down(): lax.ppermute(block, 'grow', [(i, i - 1) for i in range(1, lax.axis_size('...]
    unnamed x13 -> x11, local copies, waits for them, and re-layouts: 0.79 us -> 0.1 us
where the time goes in v3:
time: 58.8 us; the launch traced here: 58.6 us
  starting transfers between devices  22.1 us (38%)
  waiting for transfers between devices  14.4 us (24%)
  blocking collectives  11.5 us (20%)
  Pallas kernels  9.66 us (16%)
  between operations  0.77 us (1%)
    ppermute x4, starting transfers between devices, down(): lax.ppermute(block, 'grow', [(i, i - 1) for i in range(1, lax.axis_size('...  20.2 us
    ppermute x4, waiting for transfers between devices, down(): lax.ppermute(block, 'grow', [(i, i - 1) for i in range(1, lax.axis_size('...  14.4 us
    all_gather x1, blocking collectives, body(): outer = lax.all_gather(outer, 'lat', axis_index_groups=pairs, tiled=True)  11.5 us
    pallas_call x1, Pallas kernels, body(): call(upper_kernel, outs, [SMEM] + [VMEM] * 5, [room(shift + 2, fields, pa...  2.74 us
    pallas_call x1, Pallas kernels, body(): call(own_kernel, (f32(planes - 2 - shift, fields, height, width), f32(2,...  2.36 us
    ppermute x1, starting transfers between devices, body(): inner = lax.ppermute(inner, 'lat', [(i, i ^ 1) for i in range(count)])  1.92 us
    pallas_call x1, Pallas kernels, body(): call(first_kernel, f32(early, fields, height, width), [ANY] * 3, [pltpu.V...  1.76 us
    pallas_call x1, Pallas kernels, body(): call(last_kernel, outs, [SMEM] + [VMEM] * 2 + [ANY] * 2, [room(4, 2, heig...  1.46 us
  transfers between devices with their start and end apart: 5, of which 3 were waited for; matrix products, arithmetic and copies ran while one was open for 0% of the time, Pallas kernels for 11%

profile of v3, /device:TPU:6, one launch (start us, length us, event | category | flops | bytes accessed | tf_op | source)
XLA Modules:
  0.0 58.6 jit_solution(5316538166227083624)
XLA Ops:
  0.6 0.0 copy-start.2
  0.6 0.0 copy-start
  0.6 0.0 copy-start.1
  0.7 1.8 %shard_map.69 = f32[1,5,32,256]{3,2,1,0:T(8,128)} custom-call(s32[8,32,256]{2,1,0:T(8,128)} %labels.3, f32[4,8,32,256]{3,2,1,0:T(8,128)} %seed.3, f32[2,8,32,256]{3,2,1,0:T(8,128)} %potential.3), custom_call_target="tpu_custom_call" | custom-call | tf_op jit(solution)/shard_map/pallas_call | solution.py:358
  2.4 7.5 %collective-permute-start.1 = (f32[1,5,32,256]{3,2,1,0:T(8,128)}, f32[1,5,32,256]{3,2,1,0:T(8,128)S(1)}, u32[]{:S(2)}, u32[]{:S(2)}) collective-permute-start(f32[1,5,32,256]{3,2,1,0:T(8,128)} %shard_map.69), channel_id=1, source_target_pairs={{8,0},{16,8},{24,16},{32,24},{40,32},{48,40},{56,48},{64,56},{72,6... | collective-permute-start | bytes 491528 | tf_op jit(solution)/shard_map/ppermute | solution.py:335
  9.9 0.0 copy-done.2
  9.9 0.0 copy-done
  9.9 0.2 shard_map.68
  10.2 1.9 %collective-permute-start = (f32[80,256]{1,0:T(8,128)S(1)}, f32[80,256]{1,0:T(8,128)S(1)}, u32[]{:S(2)}, u32[]{:S(2)}) collective-permute-start(f32[80,256]{1,0:T(8,128)S(1)} %get-tuple-element.13), channel_id=1, source_target_pairs={{0,1},{1,0},{2,3},{3,2},{4,5},{5,4},{6,7},{7,6},{8,9},{9,8},{10,11... | collective-permute-start | bytes 245768 | tf_op jit(solution)/shard_map/ppermute | solution.py:384
  12.1 11.5 %all_gather.3.outer = f32[160,256]{1,0:T(8,128)S(1)} all-gather(f32[80,256]{1,0:T(8,128)S(1)} %get-tuple-element.14), channel_id=1, replica_groups={{1,2},{3,4},{5,6},{7,0},{9,10},{11,12},{13,14},{15,8},{17,18},{19,20},{..., dimensions={0}, use_global_device_ids=true | all-gather | bytes 245760 | tf_op jit(solution)/shard_map/all_gather | solution.py:386
  23.6 0.0 collective-permute-done.inner
  23.6 0.0 collective-permute-done.1.near
  23.6 0.1 shard_map.70
  23.7 2.9 %collective-permute-start.2 = (f32[560,256]{1,0:T(8,128)S(1)}, f32[560,256]{1,0:T(8,128)S(1)}, u32[]{:S(2)}, u32[]{:S(2)}) collective-permute-start(f32[560,256]{1,0:T(8,128)S(1)} %shard_map.70), channel_id=1, source_target_pairs={{8,0},{16,8},{24,16},{32,24},{40,32},{48,40},{56,48},{64,56},{72,6... | collective-permute-start | bytes 1720328 | tf_op jit(solution)/shard_map/ppermute | solution.py:335
  26.6 2.4 %shard_map.71 = (f32[4,5,32,256]{3,2,1,0:T(8,128)S(1)}, f32[2,5,40,256]{3,2,1,0:T(8,128)S(1)}) custom-call(f32[8,5,32,256]{3,2,1,0:T(8,128)S(1)} %get-tuple-element.12.state, f32[80,256]{1,0:T(8,128)S(1)} %collective-permute-done.inner, f32[160,256]{1,0:T(8,128)S(1)} %all_gather.3.outer), custom_call_target="tpu_custom_call" | custom-call | tf_op jit(solution)/shard_map/pallas_call | solution.py:397
  29.0 4.0 %collective-permute-start.4 = (f32[4,5,32,256]{3,2,1,0:T(8,128)S(1)}, f32[4,5,32,256]{3,2,1,0:T(8,128)S(1)}, u32[]{:S(2)}, u32[]{:S(2)}) collective-permute-start(f32[4,5,32,256]{3,2,1,0:T(8,128)S(1)} %get-tuple-element.19), channel_id=1, source_target_pairs={{8,0},{16,8},{24,16},{32,24},{40,32},{48,40},{56,48},{64,56},{72,6... | collective-permute-start | bytes 1966088 | tf_op jit(solution)/shard_map/ppermute | solution.py:335
  33.0 8.5 %collective-permute-done.2.late = f32[560,256]{1,0:T(8,128)S(1)} collective-permute-done((f32[560,256]{1,0:T(8,128)S(1)}, f32[560,256]{1,0:T(8,128)S(1)}, u32[]{:S(2)}, u32[]{:S(2)}) %collective-permute-start.2) | collective-permute-done | bytes 573472 | tf_op jit(solution)/shard_map/ppermute | solution.py:335
  41.5 1.0 %shard_map.72 = (f32[2,5,32,256]{3,2,1,0:T(8,128)S(1)}, f32[2,5,40,256]{3,2,1,0:T(8,128)S(1)}) custom-call(f32[8,5,32,256]{3,2,1,0:T(8,128)S(1)} %get-tuple-element.12.state, f32[80,256]{1,0:T(8,128)S(1)} %collective-permute-done.inner, f32[160,256]{1,0:T(8,128)S(1)} %all_gather.3.outer, f32[1,5,32,256]{3,2,1,0:T(8,128)S(1)} %collective-permute-done.1.near, ...), custom_call_target="tpu_custom_call" | custom-call | tf_op jit(solution)/shard_map/pallas_call | solution.py:405
  42.5 5.9 %collective-permute-start.3 = (f32[2,5,32,256]{3,2,1,0:T(8,128)S(1)}, f32[2,5,32,256]{3,2,1,0:T(8,128)S(1)}, u32[]{:S(2)}, u32[]{:S(2)}) collective-permute-start(f32[2,5,32,256]{3,2,1,0:T(8,128)S(1)} %get-tuple-element.17), channel_id=1, source_target_pairs={{8,0},{16,8},{24,16},{32,24},{40,32},{48,40},{56,48},{64,56},{72,6... | collective-permute-start | bytes 983048 | tf_op jit(solution)/shard_map/ppermute | solution.py:335
  48.4 0.1 copy.11.table
  48.5 5.1 %collective-permute-done.4.middle = f32[4,5,32,256]{3,2,1,0:T(8,128)S(1)} collective-permute-done((f32[4,5,32,256]{3,2,1,0:T(8,128)S(1)}, f32[4,5,32,256]{3,2,1,0:T(8,128)S(1)}, u32[]{:S(2)}, u32[]{:S(2)}) %collective-permute-start.4) | collective-permute-done | bytes 655392 | tf_op jit(solution)/shard_map/ppermute | solution.py:335
  53.6 2.7 %shard_map.73 = (f32[4,8,32,256]{3,2,1,0:T(8,128)}, f32[2,8,32,256]{3,2,1,0:T(8,128)}) custom-call(f32[16,2]{1,0:T(8,128)S(1)} %copy.11.table, f32[1,5,32,256]{3,2,1,0:T(8,128)S(1)} %collective-permute-done.1.near, f32[560,256]{1,0:T(8,128)S(1)} %collective-permute-done.2.late, f32[2,5,40,256]{3,2,1,0:T(8,128)S(1)} %get-tuple-element.18.carry, ...), custom_call_target="tpu_custom_call" | custom-call | tf_op jit(solution)/shard_map/pallas_call | solution.py:414
  56.4 0.8 %collective-permute-done.3.high = f32[2,5,32,256]{3,2,1,0:T(8,128)S(1)} collective-permute-done((f32[2,5,32,256]{3,2,1,0:T(8,128)S(1)}, f32[2,5,32,256]{3,2,1,0:T(8,128)S(1)}, u32[]{:S(2)}, u32[]{:S(2)}) %collective-permute-start.3) | collective-permute-done | bytes 327712 | tf_op jit(solution)/shard_map/ppermute | solution.py:335
  57.1 1.5 %shard_map.74 = (f32[4,8,32,256]{3,2,1,0:T(8,128)}, f32[2,8,32,256]{3,2,1,0:T(8,128)}) custom-call(f32[16,2]{1,0:T(8,128)S(1)} %copy.11.table, f32[2,5,32,256]{3,2,1,0:T(8,128)S(1)} %collective-permute-done.3.high, s32[8,32,256]{2,1,0:T(8,128)S(1)} %copy-done.3, ...), custom_call_target="tpu_custom_call", output_to_operand_aliasing={{0}: (3, {}), {1}: (4, {})} | custom-call | tf_op jit(solution)/shard_map/pallas_call | solution.py:427
  (5 shorter events, 0.0 us)
Async XLA Ops:
  0.6 9.3 %copy-start.2 = (s32[8,32,256]{2,1,0:T(8,128)S(1)}, s32[8,32,256]{2,1,0:T(8,128)}, u32[]{:S(2)}) copy-start(s32[8,32,256]{2,1,0:T(8,128)} %labels.3) | copy-start | bytes 786436
  0.6 9.3 %copy-start = (f32[4,8,32,256]{3,2,1,0:T(8,128)S(1)}, f32[4,8,32,256]{3,2,1,0:T(8,128)}, u32[]{:S(2)}) copy-start(f32[4,8,32,256]{3,2,1,0:T(8,128)} %seed.3) | copy-start | bytes 3145732
  0.6 9.3 %copy-start.1 = (f32[2,8,32,256]{3,2,1,0:T(8,128)S(1)}, f32[2,8,32,256]{3,2,1,0:T(8,128)}, u32[]{:S(2)}) copy-start(f32[2,8,32,256]{3,2,1,0:T(8,128)} %potential.3) | copy-start | bytes 1572868
  2.4 21.2 %collective-permute-start.1 = (f32[1,5,32,256]{3,2,1,0:T(8,128)}, f32[1,5,32,256]{3,2,1,0:T(8,128)S(1)}, u32[]{:S(2)}, u32[]{:S(2)}) collective-permute-start(f32[1,5,32,256]{3,2,1,0:T(8,128)} %shard_map.69), channel_id=1, source_target_pairs={{8,0},{16,8},{24,16},{32,24},{40,32},{48,40},{56,48},{64,56},{72,6... | collective-permute-start | bytes 491528 | tf_op jit(solution)/shard_map/ppermute | solution.py:335
  10.2 13.4 %collective-permute-start = (f32[80,256]{1,0:T(8,128)S(1)}, f32[80,256]{1,0:T(8,128)S(1)}, u32[]{:S(2)}, u32[]{:S(2)}) collective-permute-start(f32[80,256]{1,0:T(8,128)S(1)} %get-tuple-element.13), channel_id=1, source_target_pairs={{0,1},{1,0},{2,3},{3,2},{4,5},{5,4},{6,7},{7,6},{8,9},{9,8},{10,11... | collective-permute-start | bytes 245768 | tf_op jit(solution)/shard_map/ppermute | solution.py:384
  23.7 17.8 %collective-permute-start.2 = (f32[560,256]{1,0:T(8,128)S(1)}, f32[560,256]{1,0:T(8,128)S(1)}, u32[]{:S(2)}, u32[]{:S(2)}) collective-permute-start(f32[560,256]{1,0:T(8,128)S(1)} %shard_map.70), channel_id=1, source_target_pairs={{8,0},{16,8},{24,16},{32,24},{40,32},{48,40},{56,48},{64,56},{72,6... | collective-permute-start | bytes 1720328 | tf_op jit(solution)/shard_map/ppermute | solution.py:335
  29.0 24.7 %collective-permute-start.4 = (f32[4,5,32,256]{3,2,1,0:T(8,128)S(1)}, f32[4,5,32,256]{3,2,1,0:T(8,128)S(1)}, u32[]{:S(2)}, u32[]{:S(2)}) collective-permute-start(f32[4,5,32,256]{3,2,1,0:T(8,128)S(1)} %get-tuple-element.19), channel_id=1, source_target_pairs={{8,0},{16,8},{24,16},{32,24},{40,32},{48,40},{56,48},{64,56},{72,6... | collective-permute-start | bytes 1966088 | tf_op jit(solution)/shard_map/ppermute | solution.py:335
  41.5 6.9 %copy-start.4 = (f32[16,2]{0,1:T(2,128)S(1)}, f32[16,2]{0,1:T(2,128)}, u32[]{:S(2)}) copy-start(f32[16,2]{0,1:T(2,128)} %param.9) | copy-start | bytes 388
  41.5 12.1 %copy-start.3 = (s32[8,32,256]{2,1,0:T(8,128)S(1)}, s32[8,32,256]{2,1,0:T(8,128)}, u32[]{:S(2)}) copy-start(s32[8,32,256]{2,1,0:T(8,128)} %inflow.3) | copy-start | bytes 786436
  42.5 14.6 %collective-permute-start.3 = (f32[2,5,32,256]{3,2,1,0:T(8,128)S(1)}, f32[2,5,32,256]{3,2,1,0:T(8,128)S(1)}, u32[]{:S(2)}, u32[]{:S(2)}) collective-permute-start(f32[2,5,32,256]{3,2,1,0:T(8,128)S(1)} %get-tuple-element.17), channel_id=1, source_target_pairs={{8,0},{16,8},{24,16},{32,24},{40,32},{48,40},{56,48},{64,56},{72,6... | collective-permute-start | bytes 983048 | tf_op jit(solution)/shard_map/ppermute | solution.py:335

commit v4 on v3

--- a/solution.py
+++ b/solution.py
@@ -146,19 +146,34 @@
         edges(outer, inner)
 
 
-def pack_kernel(far, inner, outer, near, done, sems):
-    at = far.shape[0] - 2 * edge_size
+def pack_kernel(far, inner, outer, near, done, inner_out, sem):
+    at = far.shape[0] - edge_size
     slot = jnp.where(is_even(), 0, inner.shape[0])
-    copies = [
-        pltpu.make_async_copy(inner.at[0:edge_size], done.at[at : at + edge_size], sems.at[0]),
-        pltpu.make_async_copy(
-            outer.at[pl.ds(pl.multiple_of(slot, tile), edge_size)], done.at[at + edge_size :], sems.at[1]
-        ),
-    ]
-    for copy in copies:
-        copy.start()
-    for copy in copies:
-        copy.wait()
+    copy = pltpu.make_async_copy(outer.at[pl.ds(pl.multiple_of(slot, tile), edge_size)], done.at[at:], sem)
+    copy.start()
+    copy.wait()
+
+
+def rows_kernel(near, late, inner):
+    height = near.shape[2]
+
+    def edges(row):
+        for z in range(shift + 2):
+            for f in range(fields):
+                at = 2 * (z * fields + f)
+                if z < early:
+                    inner[at : at + 2, :] = near[z, f, row : row + 2, :]
+                else:
+                    first = ((z - early) * fields + f) * height + row
+                    inner[at : at + 2, :] = late[first : first + 2, :]
+
+    @pl.when(is_even())
+    def _():
+        edges(height - 2)
+
+    @pl.when(jnp.logical_not(is_even()))
+    def _():
+        edges(0)
 
 
 def gather_planes(dst, places, height):
@@ -191,14 +206,12 @@
     return [(state, z, (inner, outer), (width * z, [at + width * z for at in slots])) for z in zs]
 
 
-def upper_places(near, late, zs):
-    height = near.shape[2]
+def upper_places(near, late, inner, zs):
     width = 2 * fields
-    inner = (shift + 2 - early) * fields * height
-    outer = inner + edge_size
+    outer = (shift + 2 - early) * fields * near.shape[2]
     return [
-        (near if z < early else late, z if z < early else (z - early) * fields, (late, late),
-         (inner + width * z, [outer + width * z] * 2))
+        (near if z < early else late, z if z < early else (z - early) * fields, (inner, late),
+         (width * z, [outer + width * z] * 2))
         for z in zs
     ]
 
@@ -228,11 +241,11 @@
     carry[...] = half[count : count + 2]
 
 
-def edge_kernel(state, inner, outer, near, late, carry, done, carry_out, padded, half):
+def edge_kernel(state, inner, outer, near, late, upper_inner, carry, done, carry_out, padded, half):
     planes, height = state.shape[0], state.shape[2]
     gather_planes(
         padded,
-        own_places(state, inner, outer, range(planes - 2, planes)) + upper_places(near, late, range(2)),
+        own_places(state, inner, outer, range(planes - 2, planes)) + upper_places(near, late, upper_inner, range(2)),
         height,
     )
     one, two = steps(padded, half, done, planes, planes - 2, 2, 2, height // tile + 1)
@@ -298,12 +311,12 @@
         copy.wait()
 
 
-def upper_kernel(table, near, late, carry, middle, inflow, phase, chem, padded, half, low, liquid, sems):
+def upper_kernel(table, near, late, upper_inner, carry, middle, inflow, phase, chem, padded, half, low, liquid, sems):
     planes, height = phase.shape[1], near.shape[2]
 
     @pl.when(jnp.logical_not(is_top()))
     def _():
-        gather_planes(padded, upper_places(near, late, range(shift + 2)), height)
+        gather_planes(padded, upper_places(near, late, upper_inner, range(shift + 2)), height)
         half[0:2] = carry[...]
         one, two = steps(padded, half, low, planes, planes, 2, shift, height // tile + 1)
         one()
@@ -374,25 +387,26 @@
         start_kernel,
         (
             f32(planes, fields, height, width),
-            f32((shift + 2 - early) * fields * height + 2 * edge_size, width),
+            f32((shift + 2 - early) * fields * height + edge_size, width),
             f32(edge_rows, width),
             f32(edge_rows, width),
         ),
         [VMEM] * 3,
     )(labels, seed_blend, potential)
 
-    inner = lax.ppermute(inner, "lat", [(i, i ^ 1) for i in range(count)])
+    swap = [(i, i ^ 1) for i in range(count)]
     pairs = [[i, (i + 1) % count] for i in range(1, count, 2)]
     outer = lax.all_gather(outer, "lat", axis_index_groups=pairs, tiled=True)
-    late = call(
+    late, inner = call(
         pack_kernel,
-        jax.ShapeDtypeStruct(far.shape, far.dtype),
+        (jax.ShapeDtypeStruct(far.shape, far.dtype), jax.ShapeDtypeStruct(inner.shape, inner.dtype)),
         [ANY] * 4,
-        [pltpu.SemaphoreType.DMA((2,))],
-        ANY,
-        aliases={0: 0},
+        [pltpu.SemaphoreType.DMA],
+        (ANY, ANY),
+        aliases={0: 0, 1: 1},
     )(far, inner, outer, near)
     late = down(late)
+    inner = lax.ppermute(inner, "lat", swap)
 
     middle, carry = call(
         own_kernel,
@@ -402,19 +416,22 @@
     )(state, inner, outer)
     middle = down(middle)
 
+    upper_inner = call(rows_kernel, f32(edge_size, width), [VMEM] * 2)(near, late)
+    upper_inner = lax.ppermute(upper_inner, "lat", swap)
+
     high, carry = call(
         edge_kernel,
         (f32(2, fields, height, width), f32(2, fields, padded_rows, width)),
-        [VMEM] * 6,
+        [VMEM] * 7,
         [room(4, fields, padded_rows, width), room(4, fields, padded_rows, width)],
-    )(state, inner, outer, near, late, carry)
+    )(state, inner, outer, near, late, upper_inner, carry)
     high = down(high)
 
     outs = (f32(4, planes, height, width), f32(2, planes, height, width))
     phase, chem = call(
         upper_kernel,
         outs,
-        [SMEM] + [VMEM] * 5,
+        [SMEM] + [VMEM] * 6,
         [
             room(shift + 2, fields, padded_rows, width),
             room(shift + 2, fields, padded_rows, width),
@@ -423,7 +440,7 @@
             pltpu.SemaphoreType.DMA((2 * fields + 1,)),
         ],
         (ANY, ANY),
-    )(liquid_table, near, late, carry, middle, inflow_index)
+    )(liquid_table, near, late, upper_inner, carry, middle, inflow_index)
     return call(
         last_kernel,
         outs,

time: 58.8 us -> 57.6 us (0.980)
  waiting for transfers between devices: 14.4 us -> 10.5 us
  starting transfers between devices: 22.1 us -> 25.6 us
  blocking collectives: 11.5 us -> 10.6 us
    ppermute x4, waiting for transfers between devices: 14.4 us -> 8.07 us  [down(): lax.ppermute(block, 'grow', [(i, i - 1) for i in range(1, lax.axis_size('...]
    ppermute x1 -> x2, waiting for transfers between devices: 0.01 us -> 2.43 us  [the longest x1 1.24 us: body(): inner = lax.ppermute(inner, 'lat', swap)]
    ppermute x1 -> x2, starting transfers between devices: 1.92 us -> 3.84 us  [the longest x1 1.92 us: body(): inner = lax.ppermute(inner, 'lat', swap)]
    ppermute x4, starting transfers between devices: 20.2 us -> 21.7 us  [down(): lax.ppermute(block, 'grow', [(i, i - 1) for i in range(1, lax.axis_size('...]
    all_gather x1, blocking collectives: 11.5 us -> 10.6 us  [body(): outer = lax.all_gather(outer, 'lat', axis_index_groups=pairs, tiled=True)]
    pallas_call x2 -> x3, Pallas kernels: 2.85 us -> 2.8 us  [the longest x1 2.74 us: body(): call(upper_kernel, outs, [SMEM] + [VMEM] * 6, [room(shift + 2, fields, pa...]
  transfers between devices with their start and end apart: 5 -> 6, of which waited for: 3 -> 5; matrix products, arithmetic and copies ran while one was open for 0% -> 0% of each run, Pallas kernels for 11% -> 11%
where the time goes in v4:
time: 57.6 us; the launch traced here: 57.1 us
  starting transfers between devices  25.6 us (44%)
  blocking collectives  10.6 us (18%)
  waiting for transfers between devices  10.5 us (18%)
  Pallas kernels  9.6 us (17%)
  between operations  0.79 us (1%)
    ppermute x4, starting transfers between devices, down(): lax.ppermute(block, 'grow', [(i, i - 1) for i in range(1, lax.axis_size('...  21.7 us
    all_gather x1, blocking collectives, body(): outer = lax.all_gather(outer, 'lat', axis_index_groups=pairs, tiled=True)  10.6 us
    ppermute x4, waiting for transfers between devices, down(): lax.ppermute(block, 'grow', [(i, i - 1) for i in range(1, lax.axis_size('...  8.07 us
    pallas_call x1, Pallas kernels, body(): call(upper_kernel, outs, [SMEM] + [VMEM] * 6, [room(shift + 2, fields, pa...  2.74 us
    pallas_call x1, Pallas kernels, body(): call(own_kernel, (f32(planes - 2 - shift, fields, height, width), f32(2,...  2.36 us
    ppermute x1, starting transfers between devices, body(): inner = lax.ppermute(inner, 'lat', swap)  1.92 us
    ppermute x1, starting transfers between devices, body(): upper_inner = lax.ppermute(upper_inner, 'lat', swap)  1.92 us
    pallas_call x1, Pallas kernels, body(): call(first_kernel, f32(early, fields, height, width), [ANY] * 3, [pltpu.V...  1.76 us
  transfers between devices with their start and end apart: 6, of which 5 were waited for; matrix products, arithmetic and copies ran while one was open for 0% of the time, Pallas kernels for 11%

profile of v4, /device:TPU:6, one launch (start us, length us, event | category | flops | bytes accessed | tf_op | source)
XLA Modules:
  0.0 57.1 jit_solution(9871449291005112891)
XLA Ops:
  0.6 0.0 copy-start.2
  0.6 0.0 copy-start
  0.6 0.0 copy-start.1
  0.7 1.8 %shard_map.69 = f32[1,5,32,256]{3,2,1,0:T(8,128)} custom-call(s32[8,32,256]{2,1,0:T(8,128)} %labels.3, f32[4,8,32,256]{3,2,1,0:T(8,128)} %seed.3, f32[2,8,32,256]{3,2,1,0:T(8,128)} %potential.3), custom_call_target="tpu_custom_call" | custom-call | tf_op jit(solution)/shard_map/pallas_call | solution.py:371
  2.4 7.5 %collective-permute-start = (f32[1,5,32,256]{3,2,1,0:T(8,128)}, f32[1,5,32,256]{3,2,1,0:T(8,128)S(1)}, u32[]{:S(2)}, u32[]{:S(2)}) collective-permute-start(f32[1,5,32,256]{3,2,1,0:T(8,128)} %shard_map.69), channel_id=1, source_target_pairs={{8,0},{16,8},{24,16},{32,24},{40,32},{48,40},{56,48},{64,56},{72,6... | collective-permute-start | bytes 491528 | tf_op jit(solution)/shard_map/ppermute | solution.py:348
  9.9 0.2 shard_map.68
  10.2 10.6 %all_gather.3.outer = f32[160,256]{1,0:T(8,128)S(1)} all-gather(f32[80,256]{1,0:T(8,128)S(1)} %get-tuple-element.17), channel_id=1, replica_groups={{1,2},{3,4},{5,6},{7,0},{9,10},{11,12},{13,14},{15,8},{17,18},{19,20},{..., dimensions={0}, use_global_device_ids=true | all-gather | bytes 245760 | tf_op jit(solution)/shard_map/all_gather | solution.py:399
  20.7 0.0 collective-permute-done.near
  20.8 3.6 %collective-permute-start.2 = (f32[520,256]{1,0:T(8,128)S(1)}, f32[520,256]{1,0:T(8,128)S(1)}, u32[]{:S(2)}, u32[]{:S(2)}) collective-permute-start(f32[520,256]{1,0:T(8,128)S(1)} %get-tuple-element.19), channel_id=1, source_target_pairs={{8,0},{16,8},{24,16},{32,24},{40,32},{48,40},{56,48},{64,56},{72,6... | collective-permute-start | bytes 1597448 | tf_op jit(solution)/shard_map/ppermute | solution.py:348
  24.4 1.9 %collective-permute-start.1 = (f32[80,256]{1,0:T(8,128)S(1)}, f32[80,256]{1,0:T(8,128)S(1)}, u32[]{:S(2)}, u32[]{:S(2)}) collective-permute-start(f32[80,256]{1,0:T(8,128)S(1)} %get-tuple-element.18), channel_id=1, source_target_pairs={{0,1},{1,0},{2,3},{3,2},{4,5},{5,4},{6,7},{7,6},{8,9},{9,8},{10,11... | collective-permute-start | bytes 245768 | tf_op jit(solution)/shard_map/ppermute | solution.py:409
  26.3 1.2 %collective-permute-done.1.inner = f32[80,256]{1,0:T(8,128)S(1)} collective-permute-done((f32[80,256]{1,0:T(8,128)S(1)}, f32[80,256]{1,0:T(8,128)S(1)}, u32[]{:S(2)}, u32[]{:S(2)}) %collective-permute-start.1) | collective-permute-done | bytes 81952 | tf_op jit(solution)/shard_map/ppermute | solution.py:409
  27.6 2.4 %shard_map.72 = (f32[4,5,32,256]{3,2,1,0:T(8,128)S(1)}, f32[2,5,40,256]{3,2,1,0:T(8,128)S(1)}) custom-call(f32[8,5,32,256]{3,2,1,0:T(8,128)S(1)} %get-tuple-element.14.state, f32[80,256]{1,0:T(8,128)S(1)} %collective-permute-done.1.inner, f32[160,256]{1,0:T(8,128)S(1)} %all_gather.3.outer), custom_call_target="tpu_custom_call" | custom-call | tf_op jit(solution)/shard_map/pallas_call | solution.py:411
  29.9 3.3 %collective-permute-start.5 = (f32[4,5,32,256]{3,2,1,0:T(8,128)S(1)}, f32[4,5,32,256]{3,2,1,0:T(8,128)S(1)}, u32[]{:S(2)}, u32[]{:S(2)}) collective-permute-start(f32[4,5,32,256]{3,2,1,0:T(8,128)S(1)} %get-tuple-element.23), channel_id=1, source_target_pairs={{8,0},{16,8},{24,16},{32,24},{40,32},{48,40},{56,48},{64,56},{72,6... | collective-permute-start | bytes 1966088 | tf_op jit(solution)/shard_map/ppermute | solution.py:348
  33.2 2.1 %collective-permute-done.2.late = f32[520,256]{1,0:T(8,128)S(1)} collective-permute-done((f32[520,256]{1,0:T(8,128)S(1)}, f32[520,256]{1,0:T(8,128)S(1)}, u32[]{:S(2)}, u32[]{:S(2)}) %collective-permute-start.2) | collective-permute-done | bytes 532512 | tf_op jit(solution)/shard_map/ppermute | solution.py:348
  35.3 1.9 %collective-permute-start.3 = (f32[40,256]{1,0:T(8,128)S(1)}, f32[40,256]{1,0:T(8,128)S(1)}, u32[]{:S(2)}, u32[]{:S(2)}) collective-permute-start(f32[40,256]{1,0:T(8,128)S(1)} %shard_map.71), channel_id=1, source_target_pairs={{0,1},{1,0},{2,3},{3,2},{4,5},{5,4},{6,7},{7,6},{8,9},{9,8},{10,11... | collective-permute-start | bytes 122888 | tf_op jit(solution)/shard_map/ppermute | solution.py:420
  37.2 1.2 %collective-permute-done.3.upper_inner = f32[40,256]{1,0:T(8,128)S(1)} collective-permute-done((f32[40,256]{1,0:T(8,128)S(1)}, f32[40,256]{1,0:T(8,128)S(1)}, u32[]{:S(2)}, u32[]{:S(2)}) %collective-permute-start.3) | collective-permute-done | bytes 40992 | tf_op jit(solution)/shard_map/ppermute | solution.py:420
  38.4 1.0 %shard_map.73 = (f32[2,5,32,256]{3,2,1,0:T(8,128)S(1)}, f32[2,5,40,256]{3,2,1,0:T(8,128)S(1)}) custom-call(f32[8,5,32,256]{3,2,1,0:T(8,128)S(1)} %get-tuple-element.14.state, f32[80,256]{1,0:T(8,128)S(1)} %collective-permute-done.1.inner, f32[160,256]{1,0:T(8,128)S(1)} %all_gather.3.outer, f32[1,5,32,256]{3,2,1,0:T(8,128)S(1)} %collective-permute-done.near, ...), custom_call_target="tpu_custom_call" | custom-call | tf_op jit(solution)/shard_map/pallas_call | solution.py:422
  39.4 7.4 %collective-permute-start.4 = (f32[2,5,32,256]{3,2,1,0:T(8,128)S(1)}, f32[2,5,32,256]{3,2,1,0:T(8,128)S(1)}, u32[]{:S(2)}, u32[]{:S(2)}) collective-permute-start(f32[2,5,32,256]{3,2,1,0:T(8,128)S(1)} %get-tuple-element.21), channel_id=1, source_target_pairs={{8,0},{16,8},{24,16},{32,24},{40,32},{48,40},{56,48},{64,56},{72,6... | collective-permute-start | bytes 983048 | tf_op jit(solution)/shard_map/ppermute | solution.py:348
  46.8 0.1 copy.12.table
  46.9 2.5 %collective-permute-done.5.middle = f32[4,5,32,256]{3,2,1,0:T(8,128)S(1)} collective-permute-done((f32[4,5,32,256]{3,2,1,0:T(8,128)S(1)}, f32[4,5,32,256]{3,2,1,0:T(8,128)S(1)}, u32[]{:S(2)}, u32[]{:S(2)}) %collective-permute-start.5) | collective-permute-done | bytes 655392 | tf_op jit(solution)/shard_map/ppermute | solution.py:348
  49.4 0.0 copy-done.3
  49.4 2.7 %shard_map.74 = (f32[4,8,32,256]{3,2,1,0:T(8,128)}, f32[2,8,32,256]{3,2,1,0:T(8,128)}) custom-call(f32[16,2]{1,0:T(8,128)S(1)} %copy.12.table, f32[1,5,32,256]{3,2,1,0:T(8,128)S(1)} %collective-permute-done.near, f32[520,256]{1,0:T(8,128)S(1)} %collective-permute-done.2.late, f32[40,256]{1,0:T(8,128)S(1)} %collective-permute-done.3.upper_inner, ...), custom_call_target="tpu_custom_call" | custom-call | tf_op jit(solution)/shard_map/pallas_call | solution.py:431
  52.2 3.5 %collective-permute-done.4.high = f32[2,5,32,256]{3,2,1,0:T(8,128)S(1)} collective-permute-done((f32[2,5,32,256]{3,2,1,0:T(8,128)S(1)}, f32[2,5,32,256]{3,2,1,0:T(8,128)S(1)}, u32[]{:S(2)}, u32[]{:S(2)}) %collective-permute-start.4) | collective-permute-done | bytes 327712 | tf_op jit(solution)/shard_map/ppermute | solution.py:348
  55.7 1.5 %shard_map.75 = (f32[4,8,32,256]{3,2,1,0:T(8,128)}, f32[2,8,32,256]{3,2,1,0:T(8,128)}) custom-call(f32[16,2]{1,0:T(8,128)S(1)} %copy.12.table, f32[2,5,32,256]{3,2,1,0:T(8,128)S(1)} %collective-permute-done.4.high, s32[8,32,256]{2,1,0:T(8,128)S(1)} %copy-done.3, ...), custom_call_target="tpu_custom_call", output_to_operand_aliasing={{0}: (3, {}), {1}: (4, {})} | custom-call | tf_op jit(solution)/shard_map/pallas_call | solution.py:444
  (8 shorter events, 0.1 us)
Async XLA Ops:
  0.6 9.3 %copy-start.2 = (s32[8,32,256]{2,1,0:T(8,128)S(1)}, s32[8,32,256]{2,1,0:T(8,128)}, u32[]{:S(2)}) copy-start(s32[8,32,256]{2,1,0:T(8,128)} %labels.3) | copy-start | bytes 786436
  0.6 9.3 %copy-start = (f32[4,8,32,256]{3,2,1,0:T(8,128)S(1)}, f32[4,8,32,256]{3,2,1,0:T(8,128)}, u32[]{:S(2)}) copy-start(f32[4,8,32,256]{3,2,1,0:T(8,128)} %seed.3) | copy-start | bytes 3145732
  0.6 9.3 %copy-start.1 = (f32[2,8,32,256]{3,2,1,0:T(8,128)S(1)}, f32[2,8,32,256]{3,2,1,0:T(8,128)}, u32[]{:S(2)}) copy-start(f32[2,8,32,256]{3,2,1,0:T(8,128)} %potential.3) | copy-start | bytes 1572868
  2.4 18.3 %collective-permute-start = (f32[1,5,32,256]{3,2,1,0:T(8,128)}, f32[1,5,32,256]{3,2,1,0:T(8,128)S(1)}, u32[]{:S(2)}, u32[]{:S(2)}) collective-permute-start(f32[1,5,32,256]{3,2,1,0:T(8,128)} %shard_map.69), channel_id=1, source_target_pairs={{8,0},{16,8},{24,16},{32,24},{40,32},{48,40},{56,48},{64,56},{72,6... | collective-permute-start | bytes 491528 | tf_op jit(solution)/shard_map/ppermute | solution.py:348
  20.8 14.5 %collective-permute-start.2 = (f32[520,256]{1,0:T(8,128)S(1)}, f32[520,256]{1,0:T(8,128)S(1)}, u32[]{:S(2)}, u32[]{:S(2)}) collective-permute-start(f32[520,256]{1,0:T(8,128)S(1)} %get-tuple-element.19), channel_id=1, source_target_pairs={{8,0},{16,8},{24,16},{32,24},{40,32},{48,40},{56,48},{64,56},{72,6... | collective-permute-start | bytes 1597448 | tf_op jit(solution)/shard_map/ppermute | solution.py:348
  24.4 3.2 %collective-permute-start.1 = (f32[80,256]{1,0:T(8,128)S(1)}, f32[80,256]{1,0:T(8,128)S(1)}, u32[]{:S(2)}, u32[]{:S(2)}) collective-permute-start(f32[80,256]{1,0:T(8,128)S(1)} %get-tuple-element.18), channel_id=1, source_target_pairs={{0,1},{1,0},{2,3},{3,2},{4,5},{5,4},{6,7},{7,6},{8,9},{9,8},{10,11... | collective-permute-start | bytes 245768 | tf_op jit(solution)/shard_map/ppermute | solution.py:409
  29.9 19.5 %collective-permute-start.5 = (f32[4,5,32,256]{3,2,1,0:T(8,128)S(1)}, f32[4,5,32,256]{3,2,1,0:T(8,128)S(1)}, u32[]{:S(2)}, u32[]{:S(2)}) collective-permute-start(f32[4,5,32,256]{3,2,1,0:T(8,128)S(1)} %get-tuple-element.23), channel_id=1, source_target_pairs={{8,0},{16,8},{24,16},{32,24},{40,32},{48,40},{56,48},{64,56},{72,6... | collective-permute-start | bytes 1966088 | tf_op jit(solution)/shard_map/ppermute | solution.py:348
  35.3 3.1 %collective-permute-start.3 = (f32[40,256]{1,0:T(8,128)S(1)}, f32[40,256]{1,0:T(8,128)S(1)}, u32[]{:S(2)}, u32[]{:S(2)}) collective-permute-start(f32[40,256]{1,0:T(8,128)S(1)} %shard_map.71), channel_id=1, source_target_pairs={{0,1},{1,0},{2,3},{3,2},{4,5},{5,4},{6,7},{7,6},{8,9},{9,8},{10,11... | collective-permute-start | bytes 122888 | tf_op jit(solution)/shard_map/ppermute | solution.py:420
  38.4 8.4 %copy-start.4 = (f32[16,2]{0,1:T(2,128)S(1)}, f32[16,2]{0,1:T(2,128)}, u32[]{:S(2)}) copy-start(f32[16,2]{0,1:T(2,128)} %param.9) | copy-start | bytes 388
  38.4 11.0 %copy-start.3 = (s32[8,32,256]{2,1,0:T(8,128)S(1)}, s32[8,32,256]{2,1,0:T(8,128)}, u32[]{:S(2)}) copy-start(s32[8,32,256]{2,1,0:T(8,128)} %inflow.3) | copy-start | bytes 786436
  39.4 16.3 %collective-permute-start.4 = (f32[2,5,32,256]{3,2,1,0:T(8,128)S(1)}, f32[2,5,32,256]{3,2,1,0:T(8,128)S(1)}, u32[]{:S(2)}, u32[]{:S(2)}) collective-permute-start(f32[2,5,32,256]{3,2,1,0:T(8,128)S(1)} %get-tuple-element.21), channel_id=1, source_target_pairs={{8,0},{16,8},{24,16},{32,24},{40,32},{48,40},{56,48},{64,56},{72,6... | collective-permute-start | bytes 983048 | tf_op jit(solution)/shard_map/ppermute | solution.py:348

commit v5 on v4

--- a/solution.py
+++ b/solution.py
@@ -286,13 +286,12 @@
         copy.wait()
 
 
-def write_liquid(inflow, table, phase, chem, liquid, first, count, sems):
-    shape = (count,) + liquid.shape[2:]
-    liquid[0, 0:count] = jnp.ones(shape, jnp.float32)
-    liquid[1, 0:count] = jnp.zeros(shape, jnp.float32)
+def write_liquid(inflow, table, phase, chem, liquid, sems):
+    liquid[0] = jnp.ones(liquid.shape[1:], jnp.float32)
+    liquid[1] = jnp.zeros(liquid.shape[1:], jnp.float32)
 
     def lookup(z, _):
-        kind = inflow[first + z]
+        kind = inflow[z]
         for k in range(2):
             value = jnp.zeros(kind.shape, jnp.float32)
             for j in range(table.shape[0]):
@@ -300,11 +299,10 @@
             liquid[2 + k, z] = value
         return 0
 
-    lax.fori_loop(0, count, lookup, 0)
-    to = pl.ds(first, count)
-    pairs = [(0, phase.at[0, to])] + [(1, phase.at[a, to]) for a in range(1, 4)]
-    pairs += [(2 + k, chem.at[k, to]) for k in range(2)]
-    copies = [pltpu.make_async_copy(liquid.at[j, 0:count], dst, sems.at[i]) for i, (j, dst) in enumerate(pairs)]
+    lax.fori_loop(0, inflow.shape[0], lookup, 0)
+    pairs = [(0, phase.at[0])] + [(1, phase.at[a]) for a in range(1, 4)]
+    pairs += [(2 + k, chem.at[k]) for k in range(2)]
+    copies = [pltpu.make_async_copy(liquid.at[j], dst, sems.at[i]) for i, (j, dst) in enumerate(pairs)]
     for copy in copies:
         copy.start()
     for copy in copies:
@@ -325,19 +323,13 @@
 
     @pl.when(is_top())
     def _():
-        write_liquid(inflow, table, phase, chem, liquid, 0, planes - 2, sems)
-
-
-def last_kernel(table, high, inflow, phase_in, chem_in, phase, chem, liquid, sems):
-    planes = phase.shape[1]
-
+        write_liquid(inflow, table, phase, chem, liquid, sems)
+
+
+def last_kernel(high, phase_in, chem_in, phase, chem, extra, sems):
     @pl.when(jnp.logical_not(is_top()))
     def _():
-        write_planes([(high, planes - 2)], phase, chem, liquid.at[0], sems)
-
-    @pl.when(is_top())
-    def _():
-        write_liquid(inflow, table, phase, chem, liquid, planes - 2, 2, sems)
+        write_planes([(high, phase.shape[1] - 2)], phase, chem, extra, sems)
 
 
 def f32(*shape):
@@ -436,7 +428,7 @@
             room(shift + 2, fields, padded_rows, width),
             room(shift + 2, fields, padded_rows, width),
             room(shift, fields, height, width),
-            room(4, planes - 2, height, width),
+            room(4, planes, height, width),
             pltpu.SemaphoreType.DMA((2 * fields + 1,)),
         ],
         (ANY, ANY),
@@ -444,11 +436,11 @@
     return call(
         last_kernel,
         outs,
-        [SMEM] + [VMEM] * 2 + [ANY] * 2,
-        [room(4, 2, height, width), pltpu.SemaphoreType.DMA((fields + 1,))],
+        [VMEM] + [ANY] * 2,
+        [room(2, height, width), pltpu.SemaphoreType.DMA((fields + 1,))],
         (ANY, ANY),
-        aliases={3: 0, 4: 1},
-    )(liquid_table, high, inflow_index, phase, chem)
+        aliases={1: 0, 2: 1},
+    )(high, phase, chem)
 
 
 def solution(mesh):

time: 57.6 us -> 56.9 us (0.988)
  Pallas kernels: 9.6 us -> 8.92 us
    pallas_call x1, Pallas kernels: 1.46 us -> 0.79 us  [body(): call(last_kernel, outs, [VMEM] + [ANY] * 2, [room(2, height, width), pltp...]
where the time goes in v5:
time: 56.9 us; the launch traced here: 56.5 us
  starting transfers between devices  25.6 us (45%)
  blocking collectives  10.6 us (19%)
  waiting for transfers between devices  10.5 us (18%)
  Pallas kernels  8.92 us (16%)
  between operations  0.79 us (1%)
    ppermute x4, starting transfers between devices, down(): lax.ppermute(block, 'grow', [(i, i - 1) for i in range(1, lax.axis_size('...  21.7 us
    all_gather x1, blocking collectives, body(): outer = lax.all_gather(outer, 'lat', axis_index_groups=pairs, tiled=True)  10.6 us
    ppermute x4, waiting for transfers between devices, down(): lax.ppermute(block, 'grow', [(i, i - 1) for i in range(1, lax.axis_size('...  8.07 us
    pallas_call x1, Pallas kernels, body(): call(upper_kernel, outs, [SMEM] + [VMEM] * 6, [room(shift + 2, fields, pa...  2.74 us
    pallas_call x1, Pallas kernels, body(): call(own_kernel, (f32(planes - 2 - shift, fields, height, width), f32(2,...  2.36 us
    ppermute x1, starting transfers between devices, body(): upper_inner = lax.ppermute(upper_inner, 'lat', swap)  1.92 us
    ppermute x1, starting transfers between devices, body(): inner = lax.ppermute(inner, 'lat', swap)  1.92 us
    pallas_call x1, Pallas kernels, body(): call(first_kernel, f32(early, fields, height, width), [ANY] * 3, [pltpu.V...  1.76 us
  transfers between devices with their start and end apart: 6, of which 5 were waited for; matrix products, arithmetic and copies ran while one was open for 0% of the time, Pallas kernels for 11%

profile of v5, /device:TPU:6, one launch (start us, length us, event | category | flops | bytes accessed | tf_op | source)
XLA Modules:
  0.0 56.5 jit_solution(332151317130983892)
XLA Ops:
  0.6 0.0 copy-start.2
  0.6 0.0 copy-start
  0.6 0.0 copy-start.1
  0.7 1.8 %shard_map.69 = f32[1,5,32,256]{3,2,1,0:T(8,128)} custom-call(s32[8,32,256]{2,1,0:T(8,128)} %labels.3, f32[4,8,32,256]{3,2,1,0:T(8,128)} %seed.3, f32[2,8,32,256]{3,2,1,0:T(8,128)} %potential.3), custom_call_target="tpu_custom_call" | custom-call | tf_op jit(solution)/shard_map/pallas_call | solution.py:363
  2.4 7.5 %collective-permute-start = (f32[1,5,32,256]{3,2,1,0:T(8,128)}, f32[1,5,32,256]{3,2,1,0:T(8,128)S(1)}, u32[]{:S(2)}, u32[]{:S(2)}) collective-permute-start(f32[1,5,32,256]{3,2,1,0:T(8,128)} %shard_map.69), channel_id=1, source_target_pairs={{8,0},{16,8},{24,16},{32,24},{40,32},{48,40},{56,48},{64,56},{72,6... | collective-permute-start | bytes 491528 | tf_op jit(solution)/shard_map/ppermute | solution.py:340
  9.9 0.0 copy-done.2
  9.9 0.2 shard_map.68
  10.2 10.6 %all_gather.3.outer = f32[160,256]{1,0:T(8,128)S(1)} all-gather(f32[80,256]{1,0:T(8,128)S(1)} %get-tuple-element.17), channel_id=1, replica_groups={{1,2},{3,4},{5,6},{7,0},{9,10},{11,12},{13,14},{15,8},{17,18},{19,20},{..., dimensions={0}, use_global_device_ids=true | all-gather | bytes 245760 | tf_op jit(solution)/shard_map/all_gather | solution.py:391
  20.7 0.0 collective-permute-done.near
  20.8 3.6 %collective-permute-start.2 = (f32[520,256]{1,0:T(8,128)S(1)}, f32[520,256]{1,0:T(8,128)S(1)}, u32[]{:S(2)}, u32[]{:S(2)}) collective-permute-start(f32[520,256]{1,0:T(8,128)S(1)} %get-tuple-element.19), channel_id=1, source_target_pairs={{8,0},{16,8},{24,16},{32,24},{40,32},{48,40},{56,48},{64,56},{72,6... | collective-permute-start | bytes 1597448 | tf_op jit(solution)/shard_map/ppermute | solution.py:340
  24.4 1.9 %collective-permute-start.1 = (f32[80,256]{1,0:T(8,128)S(1)}, f32[80,256]{1,0:T(8,128)S(1)}, u32[]{:S(2)}, u32[]{:S(2)}) collective-permute-start(f32[80,256]{1,0:T(8,128)S(1)} %get-tuple-element.18), channel_id=1, source_target_pairs={{0,1},{1,0},{2,3},{3,2},{4,5},{5,4},{6,7},{7,6},{8,9},{9,8},{10,11... | collective-permute-start | bytes 245768 | tf_op jit(solution)/shard_map/ppermute | solution.py:401
  26.3 1.2 %collective-permute-done.1.inner = f32[80,256]{1,0:T(8,128)S(1)} collective-permute-done((f32[80,256]{1,0:T(8,128)S(1)}, f32[80,256]{1,0:T(8,128)S(1)}, u32[]{:S(2)}, u32[]{:S(2)}) %collective-permute-start.1) | collective-permute-done | bytes 81952 | tf_op jit(solution)/shard_map/ppermute | solution.py:401
  27.6 2.4 %shard_map.72 = (f32[4,5,32,256]{3,2,1,0:T(8,128)S(1)}, f32[2,5,40,256]{3,2,1,0:T(8,128)S(1)}) custom-call(f32[8,5,32,256]{3,2,1,0:T(8,128)S(1)} %get-tuple-element.14.state, f32[80,256]{1,0:T(8,128)S(1)} %collective-permute-done.1.inner, f32[160,256]{1,0:T(8,128)S(1)} %all_gather.3.outer), custom_call_target="tpu_custom_call" | custom-call | tf_op jit(solution)/shard_map/pallas_call | solution.py:403
  29.9 3.3 %collective-permute-start.5 = (f32[4,5,32,256]{3,2,1,0:T(8,128)S(1)}, f32[4,5,32,256]{3,2,1,0:T(8,128)S(1)}, u32[]{:S(2)}, u32[]{:S(2)}) collective-permute-start(f32[4,5,32,256]{3,2,1,0:T(8,128)S(1)} %get-tuple-element.23), channel_id=1, source_target_pairs={{8,0},{16,8},{24,16},{32,24},{40,32},{48,40},{56,48},{64,56},{72,6... | collective-permute-start | bytes 1966088 | tf_op jit(solution)/shard_map/ppermute | solution.py:340
  33.2 2.1 %collective-permute-done.2.late = f32[520,256]{1,0:T(8,128)S(1)} collective-permute-done((f32[520,256]{1,0:T(8,128)S(1)}, f32[520,256]{1,0:T(8,128)S(1)}, u32[]{:S(2)}, u32[]{:S(2)}) %collective-permute-start.2) | collective-permute-done | bytes 532512 | tf_op jit(solution)/shard_map/ppermute | solution.py:340
  35.3 1.9 %collective-permute-start.3 = (f32[40,256]{1,0:T(8,128)S(1)}, f32[40,256]{1,0:T(8,128)S(1)}, u32[]{:S(2)}, u32[]{:S(2)}) collective-permute-start(f32[40,256]{1,0:T(8,128)S(1)} %shard_map.71), channel_id=1, source_target_pairs={{0,1},{1,0},{2,3},{3,2},{4,5},{5,4},{6,7},{7,6},{8,9},{9,8},{10,11... | collective-permute-start | bytes 122888 | tf_op jit(solution)/shard_map/ppermute | solution.py:412
  37.2 1.2 %collective-permute-done.3.upper_inner = f32[40,256]{1,0:T(8,128)S(1)} collective-permute-done((f32[40,256]{1,0:T(8,128)S(1)}, f32[40,256]{1,0:T(8,128)S(1)}, u32[]{:S(2)}, u32[]{:S(2)}) %collective-permute-start.3) | collective-permute-done | bytes 40992 | tf_op jit(solution)/shard_map/ppermute | solution.py:412
  38.4 1.0 %shard_map.73 = (f32[2,5,32,256]{3,2,1,0:T(8,128)S(1)}, f32[2,5,40,256]{3,2,1,0:T(8,128)S(1)}) custom-call(f32[8,5,32,256]{3,2,1,0:T(8,128)S(1)} %get-tuple-element.14.state, f32[80,256]{1,0:T(8,128)S(1)} %collective-permute-done.1.inner, f32[160,256]{1,0:T(8,128)S(1)} %all_gather.3.outer, f32[1,5,32,256]{3,2,1,0:T(8,128)S(1)} %collective-permute-done.near, ...), custom_call_target="tpu_custom_call" | custom-call | tf_op jit(solution)/shard_map/pallas_call | solution.py:414
  39.4 7.4 %collective-permute-start.4 = (f32[2,5,32,256]{3,2,1,0:T(8,128)S(1)}, f32[2,5,32,256]{3,2,1,0:T(8,128)S(1)}, u32[]{:S(2)}, u32[]{:S(2)}) collective-permute-start(f32[2,5,32,256]{3,2,1,0:T(8,128)S(1)} %get-tuple-element.21), channel_id=1, source_target_pairs={{8,0},{16,8},{24,16},{32,24},{40,32},{48,40},{56,48},{64,56},{72,6... | collective-permute-start | bytes 983048 | tf_op jit(solution)/shard_map/ppermute | solution.py:340
  46.8 0.1 copy.11.table
  46.9 2.5 %collective-permute-done.5.middle = f32[4,5,32,256]{3,2,1,0:T(8,128)S(1)} collective-permute-done((f32[4,5,32,256]{3,2,1,0:T(8,128)S(1)}, f32[4,5,32,256]{3,2,1,0:T(8,128)S(1)}, u32[]{:S(2)}, u32[]{:S(2)}) %collective-permute-start.5) | collective-permute-done | bytes 655392 | tf_op jit(solution)/shard_map/ppermute | solution.py:340
  49.4 2.7 %shard_map.74 = (f32[4,8,32,256]{3,2,1,0:T(8,128)}, f32[2,8,32,256]{3,2,1,0:T(8,128)}) custom-call(f32[16,2]{1,0:T(8,128)S(1)} %copy.11.table, f32[1,5,32,256]{3,2,1,0:T(8,128)S(1)} %collective-permute-done.near, f32[520,256]{1,0:T(8,128)S(1)} %collective-permute-done.2.late, f32[40,256]{1,0:T(8,128)S(1)} %collective-permute-done.3.upper_inner, ...), custom_call_target="tpu_custom_call" | custom-call | tf_op jit(solution)/shard_map/pallas_call | solution.py:423
  52.2 3.5 %collective-permute-done.4.high = f32[2,5,32,256]{3,2,1,0:T(8,128)S(1)} collective-permute-done((f32[2,5,32,256]{3,2,1,0:T(8,128)S(1)}, f32[2,5,32,256]{3,2,1,0:T(8,128)S(1)}, u32[]{:S(2)}, u32[]{:S(2)}) %collective-permute-start.4) | collective-permute-done | bytes 327712 | tf_op jit(solution)/shard_map/ppermute | solution.py:340
  55.7 0.8 %shard_map.75 = (f32[4,8,32,256]{3,2,1,0:T(8,128)}, f32[2,8,32,256]{3,2,1,0:T(8,128)}) custom-call(f32[2,5,32,256]{3,2,1,0:T(8,128)S(1)} %collective-permute-done.4.high, f32[4,8,32,256]{3,2,1,0:T(8,128)} %get-tuple-element.24.phase_in, f32[2,8,32,256]{3,2,1,0:T(8,128)} %get-tuple-element.25.chem_in), custom_call_target="tpu_custom_call", output_to_operand_aliasing={{0}: (1, {}), {1}: (2, {})} | custom-call | tf_op jit(solution)/shard_map/pallas_call | solution.py:436
  (8 shorter events, 0.1 us)
Async XLA Ops:
  0.6 9.3 %copy-start.2 = (s32[8,32,256]{2,1,0:T(8,128)S(1)}, s32[8,32,256]{2,1,0:T(8,128)}, u32[]{:S(2)}) copy-start(s32[8,32,256]{2,1,0:T(8,128)} %labels.3) | copy-start | bytes 786436
  0.6 9.3 %copy-start = (f32[4,8,32,256]{3,2,1,0:T(8,128)S(1)}, f32[4,8,32,256]{3,2,1,0:T(8,128)}, u32[]{:S(2)}) copy-start(f32[4,8,32,256]{3,2,1,0:T(8,128)} %seed.3) | copy-start | bytes 3145732
  0.6 9.3 %copy-start.1 = (f32[2,8,32,256]{3,2,1,0:T(8,128)S(1)}, f32[2,8,32,256]{3,2,1,0:T(8,128)}, u32[]{:S(2)}) copy-start(f32[2,8,32,256]{3,2,1,0:T(8,128)} %potential.3) | copy-start | bytes 1572868
  2.4 18.3 %collective-permute-start = (f32[1,5,32,256]{3,2,1,0:T(8,128)}, f32[1,5,32,256]{3,2,1,0:T(8,128)S(1)}, u32[]{:S(2)}, u32[]{:S(2)}) collective-permute-start(f32[1,5,32,256]{3,2,1,0:T(8,128)} %shard_map.69), channel_id=1, source_target_pairs={{8,0},{16,8},{24,16},{32,24},{40,32},{48,40},{56,48},{64,56},{72,6... | collective-permute-start | bytes 491528 | tf_op jit(solution)/shard_map/ppermute | solution.py:340
  20.8 14.5 %collective-permute-start.2 = (f32[520,256]{1,0:T(8,128)S(1)}, f32[520,256]{1,0:T(8,128)S(1)}, u32[]{:S(2)}, u32[]{:S(2)}) collective-permute-start(f32[520,256]{1,0:T(8,128)S(1)} %get-tuple-element.19), channel_id=1, source_target_pairs={{8,0},{16,8},{24,16},{32,24},{40,32},{48,40},{56,48},{64,56},{72,6... | collective-permute-start | bytes 1597448 | tf_op jit(solution)/shard_map/ppermute | solution.py:340
  24.4 3.2 %collective-permute-start.1 = (f32[80,256]{1,0:T(8,128)S(1)}, f32[80,256]{1,0:T(8,128)S(1)}, u32[]{:S(2)}, u32[]{:S(2)}) collective-permute-start(f32[80,256]{1,0:T(8,128)S(1)} %get-tuple-element.18), channel_id=1, source_target_pairs={{0,1},{1,0},{2,3},{3,2},{4,5},{5,4},{6,7},{7,6},{8,9},{9,8},{10,11... | collective-permute-start | bytes 245768 | tf_op jit(solution)/shard_map/ppermute | solution.py:401
  29.9 19.5 %collective-permute-start.5 = (f32[4,5,32,256]{3,2,1,0:T(8,128)S(1)}, f32[4,5,32,256]{3,2,1,0:T(8,128)S(1)}, u32[]{:S(2)}, u32[]{:S(2)}) collective-permute-start(f32[4,5,32,256]{3,2,1,0:T(8,128)S(1)} %get-tuple-element.23), channel_id=1, source_target_pairs={{8,0},{16,8},{24,16},{32,24},{40,32},{48,40},{56,48},{64,56},{72,6... | collective-permute-start | bytes 1966088 | tf_op jit(solution)/shard_map/ppermute | solution.py:340
  35.3 3.1 %collective-permute-start.3 = (f32[40,256]{1,0:T(8,128)S(1)}, f32[40,256]{1,0:T(8,128)S(1)}, u32[]{:S(2)}, u32[]{:S(2)}) collective-permute-start(f32[40,256]{1,0:T(8,128)S(1)} %shard_map.71), channel_id=1, source_target_pairs={{0,1},{1,0},{2,3},{3,2},{4,5},{5,4},{6,7},{7,6},{8,9},{9,8},{10,11... | collective-permute-start | bytes 122888 | tf_op jit(solution)/shard_map/ppermute | solution.py:412
  38.4 8.4 %copy-start.4 = (f32[16,2]{0,1:T(2,128)S(1)}, f32[16,2]{0,1:T(2,128)}, u32[]{:S(2)}) copy-start(f32[16,2]{0,1:T(2,128)} %param.9) | copy-start | bytes 388
  38.4 11.0 %copy-start.3 = (s32[8,32,256]{2,1,0:T(8,128)S(1)}, s32[8,32,256]{2,1,0:T(8,128)}, u32[]{:S(2)}) copy-start(s32[8,32,256]{2,1,0:T(8,128)} %inflow.1) | copy-start | bytes 786436
  39.4 16.3 %collective-permute-start.4 = (f32[2,5,32,256]{3,2,1,0:T(8,128)S(1)}, f32[2,5,32,256]{3,2,1,0:T(8,128)S(1)}, u32[]{:S(2)}, u32[]{:S(2)}) collective-permute-start(f32[2,5,32,256]{3,2,1,0:T(8,128)S(1)} %get-tuple-element.21), channel_id=1, source_target_pairs={{8,0},{16,8},{24,16},{32,24},{40,32},{48,40},{56,48},{64,56},{72,6... | collective-permute-start | bytes 983048 | tf_op jit(solution)/shard_map/ppermute | solution.py:340

commit v6 on v5

--- a/solution.py
+++ b/solution.py
@@ -146,12 +146,10 @@
         edges(outer, inner)
 
 
-def pack_kernel(far, inner, outer, near, done, inner_out, sem):
+def pack_kernel(far, inner, outer, near, done, inner_out):
     at = far.shape[0] - edge_size
-    slot = jnp.where(is_even(), 0, inner.shape[0])
-    copy = pltpu.make_async_copy(outer.at[pl.ds(pl.multiple_of(slot, tile), edge_size)], done.at[at:], sem)
-    copy.start()
-    copy.wait()
+    slot = pl.multiple_of(jnp.where(is_even(), 0, inner.shape[0]), tile)
+    done[at:, :] = outer[pl.ds(slot, edge_size), :]
 
 
 def rows_kernel(near, late, inner):
@@ -392,9 +390,8 @@
     late, inner = call(
         pack_kernel,
         (jax.ShapeDtypeStruct(far.shape, far.dtype), jax.ShapeDtypeStruct(inner.shape, inner.dtype)),
-        [ANY] * 4,
-        [pltpu.SemaphoreType.DMA],
-        (ANY, ANY),
+        [VMEM, ANY, VMEM, ANY],
+        out_specs=(VMEM, ANY),
         aliases={0: 0, 1: 1},
     )(far, inner, outer, near)
     late = down(late)

time: 56.9 us -> 56.9 us (level)
  no operation moved by 1% of the time
where the time goes in v6:
time: 56.9 us; the launch traced here: 56.4 us
  starting transfers between devices  25.6 us (45%)
  blocking collectives  10.6 us (19%)
  waiting for transfers between devices  10.5 us (18%)
  Pallas kernels  8.88 us (16%)
  between operations  0.78 us (1%)
    ppermute x4, starting transfers between devices, down(): lax.ppermute(block, 'grow', [(i, i - 1) for i in range(1, lax.axis_size('...  21.7 us
    all_gather x1, blocking collectives, body(): outer = lax.all_gather(outer, 'lat', axis_index_groups=pairs, tiled=True)  10.6 us
    ppermute x4, waiting for transfers between devices, down(): lax.ppermute(block, 'grow', [(i, i - 1) for i in range(1, lax.axis_size('...  8.07 us
    pallas_call x1, Pallas kernels, body(): call(upper_kernel, outs, [SMEM] + [VMEM] * 6, [room(shift + 2, fields, pa...  2.74 us
    pallas_call x1, Pallas kernels, body(): call(own_kernel, (f32(planes - 2 - shift, fields, height, width), f32(2,...  2.36 us
    ppermute x1, starting transfers between devices, body(): inner = lax.ppermute(inner, 'lat', swap)  1.92 us
    ppermute x1, starting transfers between devices, body(): upper_inner = lax.ppermute(upper_inner, 'lat', swap)  1.92 us
    pallas_call x1, Pallas kernels, body(): call(first_kernel, f32(early, fields, height, width), [ANY] * 3, [pltpu.V...  1.76 us
  transfers between devices with their start and end apart: 6, of which 5 were waited for; matrix products, arithmetic and copies ran while one was open for 0% of the time, Pallas kernels for 11%

profile of v6, /device:TPU:6, one launch (start us, length us, event | category | flops | bytes accessed | tf_op | source)
XLA Modules:
  0.0 56.4 jit_solution(11524753140514221014)
XLA Ops:
  0.6 0.0 copy-start.2
  0.6 0.0 copy-start
  0.6 0.0 copy-start.1
  0.7 1.8 %shard_map.69 = f32[1,5,32,256]{3,2,1,0:T(8,128)} custom-call(s32[8,32,256]{2,1,0:T(8,128)} %labels.3, f32[4,8,32,256]{3,2,1,0:T(8,128)} %seed.3, f32[2,8,32,256]{3,2,1,0:T(8,128)} %potential.3), custom_call_target="tpu_custom_call" | custom-call | tf_op jit(solution)/shard_map/pallas_call | solution.py:361
  2.4 7.5 %collective-permute-start = (f32[1,5,32,256]{3,2,1,0:T(8,128)}, f32[1,5,32,256]{3,2,1,0:T(8,128)S(1)}, u32[]{:S(2)}, u32[]{:S(2)}) collective-permute-start(f32[1,5,32,256]{3,2,1,0:T(8,128)} %shard_map.69), channel_id=1, source_target_pairs={{8,0},{16,8},{24,16},{32,24},{40,32},{48,40},{56,48},{64,56},{72,6... | collective-permute-start | bytes 491528 | tf_op jit(solution)/shard_map/ppermute | solution.py:338
  9.9 0.2 shard_map.68
  10.2 10.6 %all_gather.3.outer = f32[160,256]{1,0:T(8,128)S(1)} all-gather(f32[80,256]{1,0:T(8,128)S(1)} %get-tuple-element.17), channel_id=1, replica_groups={{1,2},{3,4},{5,6},{7,0},{9,10},{11,12},{13,14},{15,8},{17,18},{19,20},{..., dimensions={0}, use_global_device_ids=true | all-gather | bytes 245760 | tf_op jit(solution)/shard_map/all_gather | solution.py:389
  20.7 0.0 collective-permute-done.near
  20.7 3.6 %collective-permute-start.2 = (f32[520,256]{1,0:T(8,128)S(1)}, f32[520,256]{1,0:T(8,128)S(1)}, u32[]{:S(2)}, u32[]{:S(2)}) collective-permute-start(f32[520,256]{1,0:T(8,128)S(1)} %get-tuple-element.19), channel_id=1, source_target_pairs={{8,0},{16,8},{24,16},{32,24},{40,32},{48,40},{56,48},{64,56},{72,6... | collective-permute-start | bytes 1597448 | tf_op jit(solution)/shard_map/ppermute | solution.py:338
  24.4 1.9 %collective-permute-start.1 = (f32[80,256]{1,0:T(8,128)S(1)}, f32[80,256]{1,0:T(8,128)S(1)}, u32[]{:S(2)}, u32[]{:S(2)}) collective-permute-start(f32[80,256]{1,0:T(8,128)S(1)} %get-tuple-element.18), channel_id=1, source_target_pairs={{0,1},{1,0},{2,3},{3,2},{4,5},{5,4},{6,7},{7,6},{8,9},{9,8},{10,11... | collective-permute-start | bytes 245768 | tf_op jit(solution)/shard_map/ppermute | solution.py:398
  26.3 1.2 %collective-permute-done.1.inner = f32[80,256]{1,0:T(8,128)S(1)} collective-permute-done((f32[80,256]{1,0:T(8,128)S(1)}, f32[80,256]{1,0:T(8,128)S(1)}, u32[]{:S(2)}, u32[]{:S(2)}) %collective-permute-start.1) | collective-permute-done | bytes 81952 | tf_op jit(solution)/shard_map/ppermute | solution.py:398
  27.5 2.4 %shard_map.72 = (f32[4,5,32,256]{3,2,1,0:T(8,128)S(1)}, f32[2,5,40,256]{3,2,1,0:T(8,128)S(1)}) custom-call(f32[8,5,32,256]{3,2,1,0:T(8,128)S(1)} %get-tuple-element.14.state, f32[80,256]{1,0:T(8,128)S(1)} %collective-permute-done.1.inner, f32[160,256]{1,0:T(8,128)S(1)} %all_gather.3.outer), custom_call_target="tpu_custom_call" | custom-call | tf_op jit(solution)/shard_map/pallas_call | solution.py:400
  29.9 3.3 %collective-permute-start.5 = (f32[4,5,32,256]{3,2,1,0:T(8,128)S(1)}, f32[4,5,32,256]{3,2,1,0:T(8,128)S(1)}, u32[]{:S(2)}, u32[]{:S(2)}) collective-permute-start(f32[4,5,32,256]{3,2,1,0:T(8,128)S(1)} %get-tuple-element.23), channel_id=1, source_target_pairs={{8,0},{16,8},{24,16},{32,24},{40,32},{48,40},{56,48},{64,56},{72,6... | collective-permute-start | bytes 1966088 | tf_op jit(solution)/shard_map/ppermute | solution.py:338
  33.2 2.1 %collective-permute-done.2.late = f32[520,256]{1,0:T(8,128)S(1)} collective-permute-done((f32[520,256]{1,0:T(8,128)S(1)}, f32[520,256]{1,0:T(8,128)S(1)}, u32[]{:S(2)}, u32[]{:S(2)}) %collective-permute-start.2) | collective-permute-done | bytes 532512 | tf_op jit(solution)/shard_map/ppermute | solution.py:338
  35.2 1.9 %collective-permute-start.3 = (f32[40,256]{1,0:T(8,128)S(1)}, f32[40,256]{1,0:T(8,128)S(1)}, u32[]{:S(2)}, u32[]{:S(2)}) collective-permute-start(f32[40,256]{1,0:T(8,128)S(1)} %shard_map.71), channel_id=1, source_target_pairs={{0,1},{1,0},{2,3},{3,2},{4,5},{5,4},{6,7},{7,6},{8,9},{9,8},{10,11... | collective-permute-start | bytes 122888 | tf_op jit(solution)/shard_map/ppermute | solution.py:409
  37.2 1.2 %collective-permute-done.3.upper_inner = f32[40,256]{1,0:T(8,128)S(1)} collective-permute-done((f32[40,256]{1,0:T(8,128)S(1)}, f32[40,256]{1,0:T(8,128)S(1)}, u32[]{:S(2)}, u32[]{:S(2)}) %collective-permute-start.3) | collective-permute-done | bytes 40992 | tf_op jit(solution)/shard_map/ppermute | solution.py:409
  38.4 1.0 %shard_map.73 = (f32[2,5,32,256]{3,2,1,0:T(8,128)S(1)}, f32[2,5,40,256]{3,2,1,0:T(8,128)S(1)}) custom-call(f32[8,5,32,256]{3,2,1,0:T(8,128)S(1)} %get-tuple-element.14.state, f32[80,256]{1,0:T(8,128)S(1)} %collective-permute-done.1.inner, f32[160,256]{1,0:T(8,128)S(1)} %all_gather.3.outer, f32[1,5,32,256]{3,2,1,0:T(8,128)S(1)} %collective-permute-done.near, ...), custom_call_target="tpu_custom_call" | custom-call | tf_op jit(solution)/shard_map/pallas_call | solution.py:411
  39.3 7.4 %collective-permute-start.4 = (f32[2,5,32,256]{3,2,1,0:T(8,128)S(1)}, f32[2,5,32,256]{3,2,1,0:T(8,128)S(1)}, u32[]{:S(2)}, u32[]{:S(2)}) collective-permute-start(f32[2,5,32,256]{3,2,1,0:T(8,128)S(1)} %get-tuple-element.21), channel_id=1, source_target_pairs={{8,0},{16,8},{24,16},{32,24},{40,32},{48,40},{56,48},{64,56},{72,6... | collective-permute-start | bytes 983048 | tf_op jit(solution)/shard_map/ppermute | solution.py:338
  46.8 0.1 copy.11.table
  46.8 2.5 %collective-permute-done.5.middle = f32[4,5,32,256]{3,2,1,0:T(8,128)S(1)} collective-permute-done((f32[4,5,32,256]{3,2,1,0:T(8,128)S(1)}, f32[4,5,32,256]{3,2,1,0:T(8,128)S(1)}, u32[]{:S(2)}, u32[]{:S(2)}) %collective-permute-start.5) | collective-permute-done | bytes 655392 | tf_op jit(solution)/shard_map/ppermute | solution.py:338
  49.4 0.0 copy-done.3
  49.4 2.7 %shard_map.74 = (f32[4,8,32,256]{3,2,1,0:T(8,128)}, f32[2,8,32,256]{3,2,1,0:T(8,128)}) custom-call(f32[16,2]{1,0:T(8,128)S(1)} %copy.11.table, f32[1,5,32,256]{3,2,1,0:T(8,128)S(1)} %collective-permute-done.near, f32[520,256]{1,0:T(8,128)S(1)} %collective-permute-done.2.late, f32[40,256]{1,0:T(8,128)S(1)} %collective-permute-done.3.upper_inner, ...), custom_call_target="tpu_custom_call" | custom-call | tf_op jit(solution)/shard_map/pallas_call | solution.py:420
  52.1 3.5 %collective-permute-done.4.high = f32[2,5,32,256]{3,2,1,0:T(8,128)S(1)} collective-permute-done((f32[2,5,32,256]{3,2,1,0:T(8,128)S(1)}, f32[2,5,32,256]{3,2,1,0:T(8,128)S(1)}, u32[]{:S(2)}, u32[]{:S(2)}) %collective-permute-start.4) | collective-permute-done | bytes 327712 | tf_op jit(solution)/shard_map/ppermute | solution.py:338
  55.6 0.8 %shard_map.75 = (f32[4,8,32,256]{3,2,1,0:T(8,128)}, f32[2,8,32,256]{3,2,1,0:T(8,128)}) custom-call(f32[2,5,32,256]{3,2,1,0:T(8,128)S(1)} %collective-permute-done.4.high, f32[4,8,32,256]{3,2,1,0:T(8,128)} %get-tuple-element.24.phase_in, f32[2,8,32,256]{3,2,1,0:T(8,128)} %get-tuple-element.25.chem_in), custom_call_target="tpu_custom_call", output_to_operand_aliasing={{0}: (1, {}), {1}: (2, {})} | custom-call | tf_op jit(solution)/shard_map/pallas_call | solution.py:433
  (8 shorter events, 0.0 us)
Async XLA Ops:
  0.6 9.3 %copy-start.2 = (s32[8,32,256]{2,1,0:T(8,128)S(1)}, s32[8,32,256]{2,1,0:T(8,128)}, u32[]{:S(2)}) copy-start(s32[8,32,256]{2,1,0:T(8,128)} %labels.3) | copy-start | bytes 786436
  0.6 9.3 %copy-start = (f32[4,8,32,256]{3,2,1,0:T(8,128)S(1)}, f32[4,8,32,256]{3,2,1,0:T(8,128)}, u32[]{:S(2)}) copy-start(f32[4,8,32,256]{3,2,1,0:T(8,128)} %seed.3) | copy-start | bytes 3145732
  0.6 9.3 %copy-start.1 = (f32[2,8,32,256]{3,2,1,0:T(8,128)S(1)}, f32[2,8,32,256]{3,2,1,0:T(8,128)}, u32[]{:S(2)}) copy-start(f32[2,8,32,256]{3,2,1,0:T(8,128)} %potential.3) | copy-start | bytes 1572868
  2.4 18.3 %collective-permute-start = (f32[1,5,32,256]{3,2,1,0:T(8,128)}, f32[1,5,32,256]{3,2,1,0:T(8,128)S(1)}, u32[]{:S(2)}, u32[]{:S(2)}) collective-permute-start(f32[1,5,32,256]{3,2,1,0:T(8,128)} %shard_map.69), channel_id=1, source_target_pairs={{8,0},{16,8},{24,16},{32,24},{40,32},{48,40},{56,48},{64,56},{72,6... | collective-permute-start | bytes 491528 | tf_op jit(solution)/shard_map/ppermute | solution.py:338
  20.7 14.5 %collective-permute-start.2 = (f32[520,256]{1,0:T(8,128)S(1)}, f32[520,256]{1,0:T(8,128)S(1)}, u32[]{:S(2)}, u32[]{:S(2)}) collective-permute-start(f32[520,256]{1,0:T(8,128)S(1)} %get-tuple-element.19), channel_id=1, source_target_pairs={{8,0},{16,8},{24,16},{32,24},{40,32},{48,40},{56,48},{64,56},{72,6... | collective-permute-start | bytes 1597448 | tf_op jit(solution)/shard_map/ppermute | solution.py:338
  24.4 3.2 %collective-permute-start.1 = (f32[80,256]{1,0:T(8,128)S(1)}, f32[80,256]{1,0:T(8,128)S(1)}, u32[]{:S(2)}, u32[]{:S(2)}) collective-permute-start(f32[80,256]{1,0:T(8,128)S(1)} %get-tuple-element.18), channel_id=1, source_target_pairs={{0,1},{1,0},{2,3},{3,2},{4,5},{5,4},{6,7},{7,6},{8,9},{9,8},{10,11... | collective-permute-start | bytes 245768 | tf_op jit(solution)/shard_map/ppermute | solution.py:398
  29.9 19.5 %collective-permute-start.5 = (f32[4,5,32,256]{3,2,1,0:T(8,128)S(1)}, f32[4,5,32,256]{3,2,1,0:T(8,128)S(1)}, u32[]{:S(2)}, u32[]{:S(2)}) collective-permute-start(f32[4,5,32,256]{3,2,1,0:T(8,128)S(1)} %get-tuple-element.23), channel_id=1, source_target_pairs={{8,0},{16,8},{24,16},{32,24},{40,32},{48,40},{56,48},{64,56},{72,6... | collective-permute-start | bytes 1966088 | tf_op jit(solution)/shard_map/ppermute | solution.py:338
  35.2 3.1 %collective-permute-start.3 = (f32[40,256]{1,0:T(8,128)S(1)}, f32[40,256]{1,0:T(8,128)S(1)}, u32[]{:S(2)}, u32[]{:S(2)}) collective-permute-start(f32[40,256]{1,0:T(8,128)S(1)} %shard_map.71), channel_id=1, source_target_pairs={{0,1},{1,0},{2,3},{3,2},{4,5},{5,4},{6,7},{7,6},{8,9},{9,8},{10,11... | collective-permute-start | bytes 122888 | tf_op jit(solution)/shard_map/ppermute | solution.py:409
  38.4 8.4 %copy-start.4 = (f32[16,2]{0,1:T(2,128)S(1)}, f32[16,2]{0,1:T(2,128)}, u32[]{:S(2)}) copy-start(f32[16,2]{0,1:T(2,128)} %param.9) | copy-start | bytes 388
  38.4 11.0 %copy-start.3 = (s32[8,32,256]{2,1,0:T(8,128)S(1)}, s32[8,32,256]{2,1,0:T(8,128)}, u32[]{:S(2)}) copy-start(s32[8,32,256]{2,1,0:T(8,128)} %inflow.1) | copy-start | bytes 786436
  39.3 16.3 %collective-permute-start.4 = (f32[2,5,32,256]{3,2,1,0:T(8,128)S(1)}, f32[2,5,32,256]{3,2,1,0:T(8,128)S(1)}, u32[]{:S(2)}, u32[]{:S(2)}) collective-permute-start(f32[2,5,32,256]{3,2,1,0:T(8,128)S(1)} %get-tuple-element.21), channel_id=1, source_target_pairs={{8,0},{16,8},{24,16},{32,24},{40,32},{48,40},{56,48},{64,56},{72,6... | collective-permute-start | bytes 983048 | tf_op jit(solution)/shard_map/ppermute | solution.py:338
